TPU v7x, 768 devices: a whole 4x8x12 slice. The times are simulated.
768 devices in a mesh: gx: 64 (over z_hi, y, core), gy: 12 (over z_lo, x).
Axes of the slice: x: 4, y: 8, z: 12 (z_hi: 4, z_lo: 3; z = z_hi * 3 + z_lo), core: 2. Of those that a mesh axis runs over, the one named last changes fastest.
Arguments:
- right_side: float32 [3, 128, 96, 384], P(None, 'gx', 'gy'), may hold values from -6 to 6
- face_mass: float32 [3, 128, 96, 384], P(None, 'gx', 'gy'), may hold values from 0.2 to 5
- edge_scale: float32 [3, 128, 96, 384], P(None, 'gx', None, 'gy'), may hold values from 0.1 to 0.5
- edge_mass: float32 [3, 128, 96, 384], P(None, 'gx', None, 'gy'), may hold values from 0.5 to 4
- node_scale: float32 [128, 96, 384], P('gx', None, 'gy'), may hold values from 0.1 to 0.4
Outputs:
- velocity: float32 [3, 128, 96, 384], P(None, 'gx', 'gy')
- edge_correction: float32 [3, 128, 96, 384], P(None, 'gx', None, 'gy')
All inputs are finite; a program needn't handle non-finite values.
Results may differ from a plain program's by a relative error of at most 0.00002.
Values sent between devices are 32-bit elements; how exact they have to be, the bound alone decides.
A program may use at most 32 MiB of HBM per device.

v0:
```python
import jax
import jax.numpy as jnp
from jax import lax
from jax.sharding import PartitionSpec as P

grad_div_weight = 1.0
damping = 0.3


def with_halo(cells, sides, width):
    for axis, dim in sides:
        count = lax.axis_size(axis)
        head = lax.slice_in_dim(cells, 0, width, axis=dim)
        tail = lax.slice_in_dim(cells, cells.shape[dim] - width, cells.shape[dim], axis=dim)
        cells = jnp.concatenate(
            [
                lax.ppermute(tail, axis, [(i, (i + 1) % count) for i in range(count)]),
                cells,
                lax.ppermute(head, axis, [((i + 1) % count, i) for i in range(count)]),
            ],
            axis=dim,
        )
    return cells


def forward(array_in, direction):
    return jnp.roll(array_in, -1, direction) - array_in


def backward(array_in, direction):
    return jnp.roll(array_in, 1, direction) - array_in


def face_rims(faces):
    return with_halo(faces, (("gx", 1), ("gy", 2)), 1)


def edge_rims(edges):
    return with_halo(edges, (("gx", 1), ("gy", 3)), 1)


def to_faces(edges):
    return lax.all_to_all(edges, "gy", split_axis=2, concat_axis=3, tiled=True)


def trim_faces(stacked, width):
    return stacked[:, width:-width, width:-width, :]


def trim_edges(stacked, width):
    return stacked[:, width:-width, :, width:-width]


def grad_div(padded):
    divergence = forward(padded[0], 0) + forward(padded[1], 1) + forward(padded[2], 2)
    return jnp.stack([backward(divergence, direction) for direction in range(3)])


def apply_faces(flux, face_mass):
    return face_mass * flux + grad_div_weight * trim_faces(grad_div(face_rims(flux)), 1)


def face_curl(edges):
    return jnp.stack(
        [
            forward(edges[(component + 2) % 3], (component + 1) % 3)
            - forward(edges[(component + 1) % 3], (component + 2) % 3)
            for component in range(3)
        ]
    )


def curl_adjoint(faces):
    return jnp.stack(
        [
            backward(faces[(component + 1) % 3], (component + 2) % 3)
            - backward(faces[(component + 2) % 3], (component + 1) % 3)
            for component in range(3)
        ]
    )


def gradient_adjoint(edges):
    return backward(edges[0], 0) + backward(edges[1], 1) + backward(edges[2], 2)


def node_gradient(nodal):
    return jnp.stack([forward(nodal, direction) for direction in range(3)])


def on_device(right_side, face_mass, edge_scale, edge_mass, node_scale):
    diagonal = face_mass + 2.0 * grad_div_weight
    sweep_one = damping * right_side / diagonal
    sweep_two = sweep_one + damping * (right_side - apply_faces(sweep_one, face_mass)) / diagonal
    residual = right_side - apply_faces(sweep_two, face_mass)
    edge_residual = trim_faces(curl_adjoint(face_rims(residual)), 1)
    edge_side = lax.all_to_all(edge_residual, "gy", split_axis=3, concat_axis=2, tiled=True)
    smoothed = edge_scale * edge_side
    weighted = edge_mass * smoothed
    weighted_rim = edge_rims(weighted)
    curled = trim_faces(face_curl(face_rims(to_faces(smoothed))), 1)
    potential = node_scale * -gradient_adjoint(weighted_rim)[1:-1, :, 1:-1]
    padded_potential = edge_rims(potential[None])[0]
    edge_correction = smoothed + trim_edges(node_gradient(padded_potential), 1)
    corrected = sweep_two + curled
    velocity = corrected + damping * (right_side - apply_faces(corrected, face_mass)) / diagonal
    return (velocity, edge_correction)


def solution(mesh):
    placed = (
        P(None, "gx", "gy", None),
        P(None, "gx", "gy", None),
        P(None, "gx", None, "gy"),
        P(None, "gx", None, "gy"),
        P("gx", None, "gy"),
    )
    return jax.shard_map(
        on_device,
        mesh=mesh,
        in_specs=placed,
        out_specs=(P(None, "gx", "gy", None), P(None, "gx", None, "gy")),
        check_vma=False,
    )
```

profile of v0, /device:TPU:6, one launch (start us, length us, event | category | flops | bytes accessed | tf_op | source)
XLA Modules:
  0.0 224.2 jit_solution(11937888547862640788)
XLA Ops:
  1.6 16.9 %collective-permute-start.1 = (f32[3,1,8,384]{3,2,1,0:T(8,128)S(1)}, f32[3,1,8,384]{3,2,1,0:T(8,128)S(1)}, u32[]{:S(2)}, u32[]{:S(2)}) collective-permute-start(f32[3,1,8,384]{3,2,1,0:T(8,128)S(1)} %get-tuple-element.99), channel_id=1, source_target_pairs={{12,0},{24,12},{36,24},{48,36},{60,48},{72,60},{84,72},{96,84},{10... | collective-permute-start | bytes 110600 | tf_op jit(solution)/shard_map/ppermute | solution.py:19
  20.4 8.5 %collective-permute-done = f32[3,1,8,384]{3,2,1,0:T(8,128)S(1)} collective-permute-done((f32[3,1,8,384]{3,2,1,0:T(8,128)S(1)}, f32[3,1,8,384]{3,2,1,0:T(8,128)S(1)}, u32[]{:S(2)}, u32[]{:S(2)}) %collective-permute-start) | collective-permute-done | bytes 36896 | tf_op jit(solution)/shard_map/ppermute | solution.py:17
  29.0 2.7 %collective-permute-start.3 = (f32[3,4,1,384]{3,2,1,0:T(1,128)S(1)}, f32[3,4,1,384]{3,2,1,0:T(1,128)S(1)}, u32[]{:S(2)}, u32[]{:S(2)}) collective-permute-start(f32[3,4,1,384]{3,2,1,0:T(1,128)S(1)} %get-tuple-element.59), channel_id=1, source_target_pairs={{1,0},{2,1},{3,2},{4,3},{5,4},{6,5},{7,6},{8,7},{9,8},{10,9},{11,1... | collective-permute-start | bytes 55304 | tf_op jit(solution)/shard_map/ppermute | solution.py:19
  31.8 5.2 %collective-permute-start.2 = (f32[3,4,1,384]{3,2,1,0:T(1,128)S(1)}, f32[3,4,1,384]{3,2,1,0:T(1,128)S(1)}, u32[]{:S(2)}, u32[]{:S(2)}) collective-permute-start(f32[3,4,1,384]{3,2,1,0:T(1,128)S(1)} %get-tuple-element.58), channel_id=1, source_target_pairs={{0,1},{1,2},{2,3},{3,4},{4,5},{5,6},{6,7},{7,8},{8,9},{9,10},{10,1... | collective-permute-start | bytes 55304 | tf_op jit(solution)/shard_map/ppermute | solution.py:17
  44.1 8.0 %collective-permute-done.4 = f32[3,1,8,384]{3,2,1,0:T(8,128)S(1)} collective-permute-done((f32[3,1,8,384]{3,2,1,0:T(8,128)S(1)}, f32[3,1,8,384]{3,2,1,0:T(8,128)S(1)}, u32[]{:S(2)}, u32[]{:S(2)}) %collective-permute-start.4) | collective-permute-done | bytes 36896 | tf_op jit(solution)/shard_map/ppermute | solution.py:17
  54.1 6.6 %collective-permute-start.6 = (f32[3,4,1,384]{3,2,1,0:T(1,128)S(1)}, f32[3,4,1,384]{3,2,1,0:T(1,128)S(1)}, u32[]{:S(2)}, u32[]{:S(2)}) collective-permute-start(f32[3,4,1,384]{3,2,1,0:T(1,128)S(1)} %get-tuple-element.56), channel_id=1, source_target_pairs={{0,1},{1,2},{2,3},{3,4},{4,5},{5,6},{6,7},{7,8},{8,9},{9,10},{10,1... | collective-permute-start | bytes 55304 | tf_op jit(solution)/shard_map/ppermute | solution.py:17
  67.3 8.0 %collective-permute-done.8 = f32[3,1,8,384]{3,2,1,0:T(8,128)S(1)} collective-permute-done((f32[3,1,8,384]{3,2,1,0:T(8,128)S(1)}, f32[3,1,8,384]{3,2,1,0:T(8,128)S(1)}, u32[]{:S(2)}, u32[]{:S(2)}) %collective-permute-start.8) | collective-permute-done | bytes 36896 | tf_op jit(solution)/shard_map/ppermute | solution.py:17
  75.3 5.8 %collective-permute-start.11 = (f32[3,4,1,384]{3,2,1,0:T(1,128)S(1)}, f32[3,4,1,384]{3,2,1,0:T(1,128)S(1)}, u32[]{:S(2)}, u32[]{:S(2)}) collective-permute-start(f32[3,4,1,384]{3,2,1,0:T(1,128)S(1)} %get-tuple-element.55), channel_id=1, source_target_pairs={{1,0},{2,1},{3,2},{4,3},{5,4},{6,5},{7,6},{8,7},{9,8},{10,9},{11,1... | collective-permute-start | bytes 55304 | tf_op jit(solution)/shard_map/ppermute | solution.py:19
  81.1 2.4 %collective-permute-start.10 = (f32[3,4,1,384]{3,2,1,0:T(1,128)S(1)}, f32[3,4,1,384]{3,2,1,0:T(1,128)S(1)}, u32[]{:S(2)}, u32[]{:S(2)}) collective-permute-start(f32[3,4,1,384]{3,2,1,0:T(1,128)S(1)} %get-tuple-element.54), channel_id=1, source_target_pairs={{0,1},{1,2},{2,3},{3,4},{4,5},{5,6},{6,7},{7,8},{8,9},{9,10},{10,1... | collective-permute-start | bytes 55304 | tf_op jit(solution)/shard_map/ppermute | solution.py:17
  83.5 3.2 %collective-permute-done.10 = f32[3,4,1,384]{3,2,1,0:T(1,128)S(1)} collective-permute-done((f32[3,4,1,384]{3,2,1,0:T(1,128)S(1)}, f32[3,4,1,384]{3,2,1,0:T(1,128)S(1)}, u32[]{:S(2)}, u32[]{:S(2)}) %collective-permute-start.10) | collective-permute-done | bytes 18464 | tf_op jit(solution)/shard_map/ppermute | solution.py:17
  88.0 2.5 %reshape.308 = f32[12,1,1536]{2,1,0:T(1,128)} reshape(f32[384,3,2,8]{3,2,1,0:T(2,128)S(1)} %bitcast.184) | data formatting | bytes 147456
  90.6 10.0 %all-to-all-start = ((f32[12,1,1536]{2,1,0:T(1,128)}), f32[12,1,1536]{2,1,0:T(1,128)S(1)}, u32[]{:S(2)}, u32[]{:S(2)}) async-start(f32[12,1,1536]{2,1,0:T(1,128)} %reshape.308), calls=%async_computation | async-start | bytes 147456 | tf_op jit(solution)/shard_map/all_to_all | solution.py:97
  100.9 5.3 %all-to-all-done = f32[12,1,1536]{2,1,0:T(1,128)S(1)} async-done(((f32[12,1,1536]{2,1,0:T(1,128)}), f32[12,1,1536]{2,1,0:T(1,128)S(1)}, u32[]{:S(2)}, u32[]{:S(2)}) %all-to-all-start) | async-done | bytes 73760 | tf_op jit(solution)/shard_map/all_to_all | solution.py:97
  114.8 9.0 %collective-permute-done.20 = f32[3,1,96,32]{3,2,1,0:T(8,128)S(1)} collective-permute-done((f32[3,1,96,32]{3,2,1,0:T(8,128)S(1)}, f32[3,1,96,32]{3,2,1,0:T(8,128)S(1)}, u32[]{:S(2)}, u32[]{:S(2)}) %collective-permute-start.20) | collective-permute-done | bytes 36896 | tf_op jit(solution)/shard_map/ppermute | solution.py:17
  126.8 5.8 %collective-permute-start.22 = (f32[3,4,96,1]{2,1,3,0:T(4,128)S(1)}, f32[3,4,96,1]{2,1,3,0:T(4,128)S(1)}, u32[]{:S(2)}, u32[]{:S(2)}) collective-permute-start(f32[3,4,96,1]{2,1,3,0:T(4,128)S(1)} %copy.97), channel_id=1, source_target_pairs={{0,1},{1,2},{2,3},{3,4},{4,5},{5,6},{6,7},{7,8},{8,9},{9,10},{10,1... | collective-permute-start | bytes 13832 | tf_op jit(solution)/shard_map/ppermute | solution.py:17
  138.8 7.8 %collective-permute-done.24 = f32[1,1,96,32]{2,1,3,0:T(1,128)S(1)} collective-permute-done((f32[1,1,96,32]{2,1,3,0:T(1,128)S(1)}, f32[1,1,96,32]{2,1,3,0:T(1,128)S(1)}, u32[]{:S(2)}, u32[]{:S(2)}) %collective-permute-start.24) | collective-permute-done | bytes 12320 | tf_op jit(solution)/shard_map/ppermute | solution.py:17
  149.0 5.8 %collective-permute-start.26 = (f32[1,4,96,1]{2,1,3,0:T(4,128)S(1)}, f32[1,4,96,1]{2,1,3,0:T(4,128)S(1)}, u32[]{:S(2)}, u32[]{:S(2)}) collective-permute-start(f32[1,4,96,1]{2,1,3,0:T(4,128)S(1)} %get-tuple-element.103), channel_id=1, source_target_pairs={{0,1},{1,2},{2,3},{3,4},{4,5},{5,6},{6,7},{7,8},{8,9},{9,10},{10,1... | collective-permute-start | bytes 4616 | tf_op jit(solution)/shard_map/ppermute | solution.py:17
  156.0 9.0 %all-to-all-start.1 = ((f32[12,1,1536]{2,1,0:T(1,128)}), f32[12,1,1536]{2,1,0:T(1,128)S(1)}, u32[]{:S(2)}, u32[]{:S(2)}) async-start(f32[12,1,1536]{2,1,0:T(1,128)} %reshape.310), calls=%async_computation.1 | async-start | bytes 147456 | tf_op jit(solution)/shard_map/all_to_all | solution.py:43
  165.2 5.3 %all-to-all-done.1 = f32[12,1,1536]{2,1,0:T(1,128)S(1)} async-done(((f32[12,1,1536]{2,1,0:T(1,128)}), f32[12,1,1536]{2,1,0:T(1,128)S(1)}, u32[]{:S(2)}, u32[]{:S(2)}) %all-to-all-start.1) | async-done | bytes 73760 | tf_op jit(solution)/shard_map/all_to_all | solution.py:43
  173.8 8.8 %collective-permute-start.13 = (f32[3,1,8,384]{3,2,1,0:T(8,128)S(1)}, f32[3,1,8,384]{3,2,1,0:T(8,128)S(1)}, u32[]{:S(2)}, u32[]{:S(2)}) collective-permute-start(f32[3,1,8,384]{3,2,1,0:T(8,128)S(1)} %get-tuple-element.92), channel_id=1, source_target_pairs={{12,0},{24,12},{36,24},{48,36},{60,48},{72,60},{84,72},{96,84},{10... | collective-permute-start | bytes 110600 | tf_op jit(solution)/shard_map/ppermute | solution.py:19
  187.0 5.7 %collective-permute-start.14 = (f32[3,4,1,384]{3,2,1,0:T(1,128)S(1)}, f32[3,4,1,384]{3,2,1,0:T(1,128)S(1)}, u32[]{:S(2)}, u32[]{:S(2)}) collective-permute-start(f32[3,4,1,384]{3,2,1,0:T(1,128)S(1)} %get-tuple-element.52), channel_id=1, source_target_pairs={{0,1},{1,2},{2,3},{3,4},{4,5},{5,6},{6,7},{7,8},{8,9},{9,10},{10,1... | collective-permute-start | bytes 55304 | tf_op jit(solution)/shard_map/ppermute | solution.py:17
  194.7 7.8 %collective-permute-start.17 = (f32[3,1,8,384]{3,2,1,0:T(8,128)S(1)}, f32[3,1,8,384]{3,2,1,0:T(8,128)S(1)}, u32[]{:S(2)}, u32[]{:S(2)}) collective-permute-start(f32[3,1,8,384]{3,2,1,0:T(8,128)S(1)} %get-tuple-element.91), channel_id=1, source_target_pairs={{12,0},{24,12},{36,24},{48,36},{60,48},{72,60},{84,72},{96,84},{10... | collective-permute-start | bytes 110600 | tf_op jit(solution)/shard_map/ppermute | solution.py:19
  204.6 8.3 %collective-permute-done.16 = f32[3,1,8,384]{3,2,1,0:T(8,128)S(1)} collective-permute-done((f32[3,1,8,384]{3,2,1,0:T(8,128)S(1)}, f32[3,1,8,384]{3,2,1,0:T(8,128)S(1)}, u32[]{:S(2)}, u32[]{:S(2)}) %collective-permute-start.16) | collective-permute-done | bytes 36896 | tf_op jit(solution)/shard_map/ppermute | solution.py:17
  214.9 6.4 %collective-permute-start.18 = (f32[3,4,1,384]{3,2,1,0:T(1,128)S(1)}, f32[3,4,1,384]{3,2,1,0:T(1,128)S(1)}, u32[]{:S(2)}, u32[]{:S(2)}) collective-permute-start(f32[3,4,1,384]{3,2,1,0:T(1,128)S(1)} %get-tuple-element.50), channel_id=1, source_target_pairs={{0,1},{1,2},{2,3},{3,4},{4,5},{5,6},{6,7},{7,8},{8,9},{9,10},{10,1... | collective-permute-start | bytes 55304 | tf_op jit(solution)/shard_map/ppermute | solution.py:17
  (189 shorter events, 57.5 us)
Async XLA Ops:
  1.6 18.8 %collective-permute-start.1 = (f32[3,1,8,384]{3,2,1,0:T(8,128)S(1)}, f32[3,1,8,384]{3,2,1,0:T(8,128)S(1)}, u32[]{:S(2)}, u32[]{:S(2)}) collective-permute-start(f32[3,1,8,384]{3,2,1,0:T(8,128)S(1)} %get-tuple-element.99), channel_id=1, source_target_pairs={{12,0},{24,12},{36,24},{48,36},{60,48},{72,60},{84,72},{96,84},{10... | collective-permute-start | bytes 110600 | tf_op jit(solution)/shard_map/ppermute | solution.py:19
  18.5 10.5 %collective-permute-start = (f32[3,1,8,384]{3,2,1,0:T(8,128)S(1)}, f32[3,1,8,384]{3,2,1,0:T(8,128)S(1)}, u32[]{:S(2)}, u32[]{:S(2)}) collective-permute-start(f32[3,1,8,384]{3,2,1,0:T(8,128)S(1)} %get-tuple-element.98), channel_id=1, source_target_pairs={{0,12},{12,24},{24,36},{36,48},{48,60},{60,72},{72,84},{84,96},{96... | collective-permute-start | bytes 110600 | tf_op jit(solution)/shard_map/ppermute | solution.py:17
  29.0 8.0 %collective-permute-start.3 = (f32[3,4,1,384]{3,2,1,0:T(1,128)S(1)}, f32[3,4,1,384]{3,2,1,0:T(1,128)S(1)}, u32[]{:S(2)}, u32[]{:S(2)}) collective-permute-start(f32[3,4,1,384]{3,2,1,0:T(1,128)S(1)} %get-tuple-element.59), channel_id=1, source_target_pairs={{1,0},{2,1},{3,2},{4,3},{5,4},{6,5},{7,6},{8,7},{9,8},{10,9},{11,1... | collective-permute-start | bytes 55304 | tf_op jit(solution)/shard_map/ppermute | solution.py:19
  41.7 10.4 %collective-permute-start.4 = (f32[3,1,8,384]{3,2,1,0:T(8,128)S(1)}, f32[3,1,8,384]{3,2,1,0:T(8,128)S(1)}, u32[]{:S(2)}, u32[]{:S(2)}) collective-permute-start(f32[3,1,8,384]{3,2,1,0:T(8,128)S(1)} %get-tuple-element.96), channel_id=1, source_target_pairs={{0,12},{12,24},{24,36},{36,48},{48,60},{60,72},{72,84},{84,96},{96... | collective-permute-start | bytes 110600 | tf_op jit(solution)/shard_map/ppermute | solution.py:17
  52.1 8.6 %collective-permute-start.7 = (f32[3,4,1,384]{3,2,1,0:T(1,128)S(1)}, f32[3,4,1,384]{3,2,1,0:T(1,128)S(1)}, u32[]{:S(2)}, u32[]{:S(2)}) collective-permute-start(f32[3,4,1,384]{3,2,1,0:T(1,128)S(1)} %get-tuple-element.57), channel_id=1, source_target_pairs={{1,0},{2,1},{3,2},{4,3},{5,4},{6,5},{7,6},{8,7},{9,8},{10,9},{11,1... | collective-permute-start | bytes 55304 | tf_op jit(solution)/shard_map/ppermute | solution.py:19
  54.1 8.1 %collective-permute-start.6 = (f32[3,4,1,384]{3,2,1,0:T(1,128)S(1)}, f32[3,4,1,384]{3,2,1,0:T(1,128)S(1)}, u32[]{:S(2)}, u32[]{:S(2)}) collective-permute-start(f32[3,4,1,384]{3,2,1,0:T(1,128)S(1)} %get-tuple-element.56), channel_id=1, source_target_pairs={{0,1},{1,2},{2,3},{3,4},{4,5},{5,6},{6,7},{7,8},{8,9},{9,10},{10,1... | collective-permute-start | bytes 55304 | tf_op jit(solution)/shard_map/ppermute | solution.py:17
  64.8 10.4 %collective-permute-start.8 = (f32[3,1,8,384]{3,2,1,0:T(8,128)S(1)}, f32[3,1,8,384]{3,2,1,0:T(8,128)S(1)}, u32[]{:S(2)}, u32[]{:S(2)}) collective-permute-start(f32[3,1,8,384]{3,2,1,0:T(8,128)S(1)} %get-tuple-element.94), channel_id=1, source_target_pairs={{0,12},{12,24},{24,36},{36,48},{48,60},{60,72},{72,84},{84,96},{96... | collective-permute-start | bytes 110600 | tf_op jit(solution)/shard_map/ppermute | solution.py:17
  75.3 8.3 %collective-permute-start.11 = (f32[3,4,1,384]{3,2,1,0:T(1,128)S(1)}, f32[3,4,1,384]{3,2,1,0:T(1,128)S(1)}, u32[]{:S(2)}, u32[]{:S(2)}) collective-permute-start(f32[3,4,1,384]{3,2,1,0:T(1,128)S(1)} %get-tuple-element.55), channel_id=1, source_target_pairs={{1,0},{2,1},{3,2},{4,3},{5,4},{6,5},{7,6},{8,7},{9,8},{10,9},{11,1... | collective-permute-start | bytes 55304 | tf_op jit(solution)/shard_map/ppermute | solution.py:19
  90.6 15.6 %all-to-all-start = ((f32[12,1,1536]{2,1,0:T(1,128)}), f32[12,1,1536]{2,1,0:T(1,128)S(1)}, u32[]{:S(2)}, u32[]{:S(2)}) async-start(f32[12,1,1536]{2,1,0:T(1,128)} %reshape.308), calls=%async_computation | async-start | bytes 147456 | tf_op jit(solution)/shard_map/all_to_all | solution.py:97
  111.8 12.0 %collective-permute-start.20 = (f32[3,1,96,32]{3,2,1,0:T(8,128)S(1)}, f32[3,1,96,32]{3,2,1,0:T(8,128)S(1)}, u32[]{:S(2)}, u32[]{:S(2)}) collective-permute-start(f32[3,1,96,32]{3,2,1,0:T(8,128)S(1)} %get-tuple-element.20), channel_id=1, source_target_pairs={{0,12},{12,24},{24,36},{36,48},{48,60},{60,72},{72,84},{84,96},{96... | collective-permute-start | bytes 110600 | tf_op jit(solution)/shard_map/ppermute | solution.py:17
  124.3 8.5 %collective-permute-start.23 = (f32[3,4,96,1]{2,1,3,0:T(4,128)S(1)}, f32[3,4,96,1]{2,1,3,0:T(4,128)S(1)}, u32[]{:S(2)}, u32[]{:S(2)}) collective-permute-start(f32[3,4,96,1]{2,1,3,0:T(4,128)S(1)} %copy.98), channel_id=1, source_target_pairs={{1,0},{2,1},{3,2},{4,3},{5,4},{6,5},{7,6},{8,7},{9,8},{10,9},{11,1... | collective-permute-start | bytes 13832 | tf_op jit(solution)/shard_map/ppermute | solution.py:19
  126.8 7.2 %collective-permute-start.22 = (f32[3,4,96,1]{2,1,3,0:T(4,128)S(1)}, f32[3,4,96,1]{2,1,3,0:T(4,128)S(1)}, u32[]{:S(2)}, u32[]{:S(2)}) collective-permute-start(f32[3,4,96,1]{2,1,3,0:T(4,128)S(1)} %copy.97), channel_id=1, source_target_pairs={{0,1},{1,2},{2,3},{3,4},{4,5},{5,6},{6,7},{7,8},{8,9},{9,10},{10,1... | collective-permute-start | bytes 13832 | tf_op jit(solution)/shard_map/ppermute | solution.py:17
  136.4 10.2 %collective-permute-start.24 = (f32[1,1,96,32]{2,1,3,0:T(1,128)S(1)}, f32[1,1,96,32]{2,1,3,0:T(1,128)S(1)}, u32[]{:S(2)}, u32[]{:S(2)}) collective-permute-start(f32[1,1,96,32]{2,1,3,0:T(1,128)S(1)} %get-tuple-element.105), channel_id=1, source_target_pairs={{0,12},{12,24},{24,36},{36,48},{48,60},{60,72},{72,84},{84,96},{96... | collective-permute-start | bytes 36872 | tf_op jit(solution)/shard_map/ppermute | solution.py:17
  146.6 18.4 %collective-permute-start.27 = (f32[1,4,96,1]{2,1,3,0:T(4,128)S(1)}, f32[1,4,96,1]{2,1,3,0:T(4,128)S(1)}, u32[]{:S(2)}, u32[]{:S(2)}) collective-permute-start(f32[1,4,96,1]{2,1,3,0:T(4,128)S(1)} %get-tuple-element.104), channel_id=1, source_target_pairs={{1,0},{2,1},{3,2},{4,3},{5,4},{6,5},{7,6},{8,7},{9,8},{10,9},{11,1... | collective-permute-start | bytes 4616 | tf_op jit(solution)/shard_map/ppermute | solution.py:19
  149.0 16.0 %collective-permute-start.26 = (f32[1,4,96,1]{2,1,3,0:T(4,128)S(1)}, f32[1,4,96,1]{2,1,3,0:T(4,128)S(1)}, u32[]{:S(2)}, u32[]{:S(2)}) collective-permute-start(f32[1,4,96,1]{2,1,3,0:T(4,128)S(1)} %get-tuple-element.103), channel_id=1, source_target_pairs={{0,1},{1,2},{2,3},{3,4},{4,5},{5,6},{6,7},{7,8},{8,9},{9,10},{10,1... | collective-permute-start | bytes 4616 | tf_op jit(solution)/shard_map/ppermute | solution.py:17
  156.0 14.5 %all-to-all-start.1 = ((f32[12,1,1536]{2,1,0:T(1,128)}), f32[12,1,1536]{2,1,0:T(1,128)S(1)}, u32[]{:S(2)}, u32[]{:S(2)}) async-start(f32[12,1,1536]{2,1,0:T(1,128)} %reshape.310), calls=%async_computation.1 | async-start | bytes 147456 | tf_op jit(solution)/shard_map/all_to_all | solution.py:43
  171.9 10.7 %collective-permute-start.12 = (f32[3,1,8,384]{3,2,1,0:T(8,128)S(1)}, f32[3,1,8,384]{3,2,1,0:T(8,128)S(1)}, u32[]{:S(2)}, u32[]{:S(2)}) collective-permute-start(f32[3,1,8,384]{3,2,1,0:T(8,128)S(1)} %get-tuple-element.93), channel_id=1, source_target_pairs={{0,12},{12,24},{24,36},{36,48},{48,60},{60,72},{72,84},{84,96},{96... | collective-permute-start | bytes 110600 | tf_op jit(solution)/shard_map/ppermute | solution.py:17
  173.8 10.9 %collective-permute-start.13 = (f32[3,1,8,384]{3,2,1,0:T(8,128)S(1)}, f32[3,1,8,384]{3,2,1,0:T(8,128)S(1)}, u32[]{:S(2)}, u32[]{:S(2)}) collective-permute-start(f32[3,1,8,384]{3,2,1,0:T(8,128)S(1)} %get-tuple-element.92), channel_id=1, source_target_pairs={{12,0},{24,12},{36,24},{48,36},{60,48},{72,60},{84,72},{96,84},{10... | collective-permute-start | bytes 110600 | tf_op jit(solution)/shard_map/ppermute | solution.py:19
  184.7 8.3 %collective-permute-start.15 = (f32[3,4,1,384]{3,2,1,0:T(1,128)S(1)}, f32[3,4,1,384]{3,2,1,0:T(1,128)S(1)}, u32[]{:S(2)}, u32[]{:S(2)}) collective-permute-start(f32[3,4,1,384]{3,2,1,0:T(1,128)S(1)} %get-tuple-element.53), channel_id=1, source_target_pairs={{1,0},{2,1},{3,2},{4,3},{5,4},{6,5},{7,6},{8,7},{9,8},{10,9},{11,1... | collective-permute-start | bytes 55304 | tf_op jit(solution)/shard_map/ppermute | solution.py:19
  187.0 7.1 %collective-permute-start.14 = (f32[3,4,1,384]{3,2,1,0:T(1,128)S(1)}, f32[3,4,1,384]{3,2,1,0:T(1,128)S(1)}, u32[]{:S(2)}, u32[]{:S(2)}) collective-permute-start(f32[3,4,1,384]{3,2,1,0:T(1,128)S(1)} %get-tuple-element.52), channel_id=1, source_target_pairs={{0,1},{1,2},{2,3},{3,4},{4,5},{5,6},{6,7},{7,8},{8,9},{9,10},{10,1... | collective-permute-start | bytes 55304 | tf_op jit(solution)/shard_map/ppermute | solution.py:17
  194.7 9.9 %collective-permute-start.17 = (f32[3,1,8,384]{3,2,1,0:T(8,128)S(1)}, f32[3,1,8,384]{3,2,1,0:T(8,128)S(1)}, u32[]{:S(2)}, u32[]{:S(2)}) collective-permute-start(f32[3,1,8,384]{3,2,1,0:T(8,128)S(1)} %get-tuple-element.91), channel_id=1, source_target_pairs={{12,0},{24,12},{36,24},{48,36},{60,48},{72,60},{84,72},{96,84},{10... | collective-permute-start | bytes 110600 | tf_op jit(solution)/shard_map/ppermute | solution.py:19
  202.5 10.4 %collective-permute-start.16 = (f32[3,1,8,384]{3,2,1,0:T(8,128)S(1)}, f32[3,1,8,384]{3,2,1,0:T(8,128)S(1)}, u32[]{:S(2)}, u32[]{:S(2)}) collective-permute-start(f32[3,1,8,384]{3,2,1,0:T(8,128)S(1)} %get-tuple-element.90), channel_id=1, source_target_pairs={{0,12},{12,24},{24,36},{36,48},{48,60},{60,72},{72,84},{84,96},{96... | collective-permute-start | bytes 110600 | tf_op jit(solution)/shard_map/ppermute | solution.py:17
  213.0 9.4 %collective-permute-start.19 = (f32[3,4,1,384]{3,2,1,0:T(1,128)S(1)}, f32[3,4,1,384]{3,2,1,0:T(1,128)S(1)}, u32[]{:S(2)}, u32[]{:S(2)}) collective-permute-start(f32[3,4,1,384]{3,2,1,0:T(1,128)S(1)} %get-tuple-element.51), channel_id=1, source_target_pairs={{1,0},{2,1},{3,2},{4,3},{5,4},{6,5},{7,6},{8,7},{9,8},{10,9},{11,1... | collective-permute-start | bytes 55304 | tf_op jit(solution)/shard_map/ppermute | solution.py:19
  214.9 7.9 %collective-permute-start.18 = (f32[3,4,1,384]{3,2,1,0:T(1,128)S(1)}, f32[3,4,1,384]{3,2,1,0:T(1,128)S(1)}, u32[]{:S(2)}, u32[]{:S(2)}) collective-permute-start(f32[3,4,1,384]{3,2,1,0:T(1,128)S(1)} %get-tuple-element.50), channel_id=1, source_target_pairs={{0,1},{1,2},{2,3},{3,4},{4,5},{5,6},{6,7},{7,8},{8,9},{9,10},{10,1... | collective-permute-start | bytes 55304 | tf_op jit(solution)/shard_map/ppermute | solution.py:17
  (13 other events, 77.3 us)
where the time goes:
time: 227 us; the launch traced here: 224 us
  starting transfers between devices  133 us (59%)
  waiting for transfers between devices  71.5 us (31%)
  local copies, waits for them, and re-layouts  12.2 us (5%)
  other arithmetic  5.79 us (3%)
    ppermute x14, starting transfers between devices, with_halo(): lax.ppermute(head, axis, [((i + 1) % count, i) for i in range(count)])  60.5 us
    ppermute x14, waiting for transfers between devices, with_halo(): lax.ppermute(tail, axis, [(i, (i + 1) % count) for i in range(count)])  58.2 us
    ppermute x14, starting transfers between devices, with_halo(): lax.ppermute(tail, axis, [(i, (i + 1) % count) for i in range(count)])  53.4 us
    all_to_all x1, starting transfers between devices, on_device(): lax.all_to_all(edge_residual, 'gy', split_axis=3, concat_axis=2, tiled=True)  10 us
    all_to_all x1, starting transfers between devices, to_faces(): return lax.all_to_all(edges, 'gy', split_axis=2, concat_axis=3, tiled=True)  8.99 us
    unnamed x22, local copies, waits for them, and re-layouts  7.3 us
    all_to_all x1, waiting for transfers between devices, to_faces(): return lax.all_to_all(edges, 'gy', split_axis=2, concat_axis=3, tiled=True)  5.33 us
    all_to_all x1, waiting for transfers between devices, on_device(): lax.all_to_all(edge_residual, 'gy', split_axis=3, concat_axis=2, tiled=True)  5.27 us
  transfers between devices with their start and end apart: 30, of which 16 were waited for; matrix products, arithmetic and copies ran while one was open for 2% of the time, Pallas kernels for 0%

commit v1 on v0

v1 whole, which is shorter than its diff:
```python
import functools

import jax
import jax.numpy as jnp
from jax import lax
from jax.experimental import pallas as pl
from jax.experimental.pallas import tpu as pltpu
from jax.sharding import PartitionSpec as P

MESH = pl.DeviceIdType.MESH
grad_div_weight = 1.0
damping = 0.3


def z_up(a):
    return pltpu.roll(a, a.shape[-1] - 1, axis=a.ndim - 1)


def z_down(a):
    return pltpu.roll(a, 1, axis=a.ndim - 1)


def y_up(a):
    return pltpu.roll(a, a.shape[-2] - 1, axis=a.ndim - 2)


def y_down(a):
    return pltpu.roll(a, 1, axis=a.ndim - 2)


def half_turn(a):
    return pltpu.roll(a, 4, axis=a.ndim - 2)


def sublane(shape):
    return lax.broadcasted_iota(jnp.int32, shape, len(shape) - 2)


def pack_halves(parts, upper):
    low = sublane(parts[0].shape) < 4
    packed = []
    for i in range(0, len(parts), 2):
        a = parts[i]
        b = half_turn(parts[i + 1] if i + 1 < len(parts) else a)
        packed.append(jnp.where(low, b, a) if upper else jnp.where(low, a, b))
    return packed


def halo_tiles(from_below, from_above, i):
    a, b = from_below[i // 2], from_above[i // 2]
    low = sublane(a.shape) < 4
    if i % 2 == 0:
        return jnp.where(low, b, a)
    return half_turn(jnp.where(low, a, b))


def kernel(n_gx, n_gy, r_ref, fm_ref, es_ref, em_ref, ns_ref, vel_ref, ec_ref,
           x_right, x_left, y_upper, y_lower, cr_upper, cr_lower, cl_upper, cl_lower, edge_out, back_out,
           in_left, in_right, in_below, in_above, in_cl_below, in_cl_above, in_cr_below, in_cr_above,
           edge_in, back_in, faced, ef_right, ef_left, in_ef_left, in_ef_right,
           res_right, res_left, in_res_left, in_res_right, s2_ref, div2_ref, res_ref, send_sem, recv_sem):
    gx, gy = lax.axis_index("gx"), lax.axis_index("gy")

    def at(dx, dy):
        return (lax.rem(gx + dx + n_gx, n_gx), lax.rem(gy + dy + n_gy, n_gy))

    barrier = pltpu.get_barrier_semaphore()
    greeted = [at(0, j) for j in range(1, n_gy)] + [at(a, b) for a in (1, -1) for b in (-1, 0, 1)]
    for peer in greeted:
        pl.semaphore_signal(barrier, inc=1, device_id=peer, device_id_type=MESH)

    def message(index, src, dst, peer):
        return pltpu.make_async_remote_copy(
            src_ref=src, dst_ref=dst, send_sem=send_sem.at[index], recv_sem=recv_sem.at[index],
            device_id=peer, device_id_type=MESH)

    r = [[r_ref[c, p] for p in range(2)] for c in range(3)]
    fm = [[fm_ref[c, p] for p in range(2)] for c in range(3)]
    s1 = [[damping * r[c][p] / (fm[c][p] + 2.0 * grad_div_weight) for p in range(2)] for c in range(3)]
    to_right = [r[0][1], r[1][1], r[2][1], fm[0][1], fm[1][1], fm[2][1], s1[0][0], s1[1][0], s1[2][0]]
    to_left = [r[0][0], fm[0][0], s1[1][0], s1[2][0], s1[0][1]]
    own = [f[c][p] for f in (r, fm) for c in range(3) for p in range(2)]
    for ref, parts in ((x_right, to_right), (x_left, to_left),
                       (y_upper, pack_halves(own, True)), (y_lower, pack_halves(own, False)),
                       (cr_upper, pack_halves(to_right, True)), (cr_lower, pack_halves(to_right, False)),
                       (cl_upper, pack_halves(to_left, True)), (cl_lower, pack_halves(to_left, False))):
        for i, part in enumerate(parts):
            ref[i] = part

    rows, width = es_ref.shape[2], es_ref.shape[3]
    low96 = sublane((rows, width)) % 8 < 4
    for a in range(7):
        windows = []
        for p in range(2):
            field = es_ref[a, p] if a < 3 else em_ref[a - 3, p] if a < 6 else ns_ref[p]
            after = jnp.concatenate([field[8:], field[:8]], axis=0)
            before = jnp.concatenate([field[rows - 8:], field[:rows - 8]], axis=0)
            windows += [field, jnp.where(low96, after, before)]
        edge_out[:, a] = jnp.concatenate(windows, axis=1).reshape(n_gy, 8, 4 * width)

    pl.semaphore_wait(barrier, len(greeted))

    first = [
        message(4, cr_upper, in_cl_below, at(1, 1)), message(5, cr_lower, in_cl_above, at(1, -1)),
        message(6, cl_upper, in_cr_below, at(-1, 1)), message(7, cl_lower, in_cr_above, at(-1, -1)),
        message(0, x_right, in_left, at(1, 0)), message(1, x_left, in_right, at(-1, 0)),
        message(2, y_upper, in_below, at(0, 1)), message(3, y_lower, in_above, at(0, -1)),
    ]
    for copy in first:
        copy.start()
    exchange = []
    for j in range(1, n_gy):
        peer = at(0, j)
        exchange.append(message(7 + j, edge_out.at[peer[1]], edge_in.at[gy], peer))
    for copy in exchange:
        copy.start()
    edge_in[gy] = edge_out[gy]

    for copy in exchange:
        copy.wait_recv()
    lane4 = lax.broadcasted_iota(jnp.int32, (8, 128), 1) // width
    for p in range(2):
        for a in range(7):
            for h in range(2):
                q = 2 * p + h
                for m in range(3):
                    tile = None
                    for jj in range(4):
                        piece = edge_in[4 * m + jj, a]
                        if jj != q:
                            piece = pltpu.roll(piece, (width * (jj - q)) % 128, axis=1)
                        tile = piece if tile is None else jnp.where(lane4 == jj, piece, tile)
                    faced[p, a, 8 * h:8 * h + 8, 128 * m:128 * m + 128] = tile
    sub = sublane((8, r_ref.shape[3]))
    for ref, p, count in ((ef_right, 1, 4), (ef_left, 0, 7)):
        for a in range(count):
            ref[a] = faced[p, a, 0:8]
        for base in range(0, count, 4):
            tile = None
            for i in range(min(4, count - base)):
                piece = faced[p, base + i, 8:16]
                piece = piece if i == 0 else pltpu.roll(piece, 2 * i, axis=0)
                tile = piece if i == 0 else jnp.where((sub == 2 * i) | (sub == 2 * i - 1), piece, tile)
            ref[count + base // 4] = tile
    edge_halo = [message(19, ef_right, in_ef_left, at(1, 0)), message(20, ef_left, in_ef_right, at(-1, 0))]
    for copy in edge_halo:
        copy.start()

    for copy in first:
        copy.wait_recv()

    def joined(own_part, halo):
        return jnp.concatenate([own_part, halo], axis=0)

    def left(i):
        return joined(in_left[i], halo_tiles(in_cl_below, in_cl_above, i))

    def right(i):
        return joined(in_right[i], halo_tiles(in_cr_below, in_cr_above, i))

    def mine(i, part):
        return joined(part, halo_tiles(in_below, in_above, i))

    rr = {(c, p): mine(2 * c + p, r_ref[c, p]) for c in range(3) for p in range(2)}
    ff = {(c, p): mine(6 + 2 * c + p, fm_ref[c, p]) for c in range(3) for p in range(2)}
    for c in range(3):
        rr[c, -1], ff[c, -1] = left(c), left(3 + c)
    rr[0, 2], ff[0, 2] = right(0), right(1)
    dd = {key: ff[key] + 2.0 * grad_div_weight for key in ff}
    ss = {key: damping * rr[key] / dd[key] for key in rr}
    for c in range(3):
        ss[c, -2] = left(6 + c)
    ss[1, 2], ss[2, 2], ss[0, 3] = right(2), right(3), right(4)

    def divergence(u, p):
        return (u[0, p + 1] - u[0, p]) + (y_up(u[1, p]) - u[1, p]) + (z_up(u[2, p]) - u[2, p])

    def back_of(div, c, p):
        shifted = div[p - 1] if c == 0 else y_down(div[p]) if c == 1 else z_down(div[p])
        return shifted - div[p]

    def apply_faces(u, div, c, p):
        return ff[c, p] * u[c, p] + grad_div_weight * back_of(div, c, p)

    div1 = {p: divergence(ss, p) for p in range(-2, 3)}
    tt = {key: ss[key] + damping * (rr[key] - apply_faces(ss, div1, *key)) / dd[key] for key in rr}
    div2 = {p: divergence(tt, p) for p in range(-1, 2)}
    res = {(c, p): rr[c, p] - apply_faces(tt, div2, c, p) for c in range(3) for p in range(2)}

    def pack_three_rows(parts):
        packed = []
        middle = (sub >= 2) & (sub <= 4)
        for i in range(0, len(parts), 2):
            a = parts[i][8:16]
            packed.append(jnp.where(middle, half_turn(parts[i + 1][8:16]), a) if i + 1 < len(parts) else a)
        return packed

    right_going = [res[1, 0], res[2, 0], res[0, 1], res[1, 1], res[2, 1]]
    left_going = [res[0, 0], res[1, 0], res[2, 0]]
    for ref, parts in ((res_right, right_going), (res_left, left_going)):
        for i, part in enumerate([a[0:8] for a in parts] + pack_three_rows(parts)):
            ref[i] = part
    second = [message(21, res_right, in_res_left, at(1, 0)), message(22, res_left, in_res_right, at(-1, 0))]
    for copy in second:
        copy.start()
    for copy in edge_halo:
        copy.wait_recv()
    for copy in second:
        copy.wait_recv()

    def res_halo(ref, count, i):
        tile = ref[count + i // 2]
        return joined(ref[i], half_turn(tile) if i % 2 else tile)

    for i, key in enumerate(((1, -2), (2, -2), (0, -1), (1, -1), (2, -1))):
        res[key] = res_halo(in_res_left, 5, i)
    for c in range(3):
        res[c, 2] = res_halo(in_res_right, 3, c)

    def ef_halo(ref, count, i):
        tile = ref[count + i // 4]
        return joined(ref[i], pltpu.roll(tile, 8 - 2 * (i % 4), axis=0) if i % 4 else tile)

    edge = {(a, p): faced[p, a] for a in range(7) for p in range(2)}
    for a in range(4):
        edge[a, -1] = ef_halo(in_ef_left, 4, a)
    for a in range(7):
        edge[a, 2] = ef_halo(in_ef_right, 7, a)

    def shift_down(u, c, p, direction):
        return u[c, p - 1] if direction == 0 else y_down(u[c, p]) if direction == 1 else z_down(u[c, p])

    def edge_residual(a, p):
        b, c = (a + 1) % 3, (a + 2) % 3
        return (shift_down(res, b, p, c) - res[b, p]) - (shift_down(res, c, p, b) - res[c, p])

    sm = {(a, p): edge[a, p] * edge_residual(a, p) for p in range(-1, 3) for a in range(3)}
    ww = {(a, p): edge[3 + a, p] * sm[a, p] for p in range(-1, 3) for a in range(3) if p >= 0 or a == 0}
    pot = {}
    for p in range(3):
        adjoint = ((ww[0, p - 1] - ww[0, p]) + (y_down(ww[1, p]) - ww[1, p])) + (z_down(ww[2, p]) - ww[2, p])
        pot[p] = edge[6, p] * -adjoint
    lane = lax.broadcasted_iota(jnp.int32, (8, 128), 1) // width
    corr = []
    for c in range(3):
        for p in range(2):
            ahead = pot[p + 1] if c == 0 else y_up(pot[p]) if c == 1 else z_up(pot[p])
            corr.append((sm[c, p] + (ahead - pot[p]))[0:8])
    for k in range(n_gy):
        for t in range(2):
            tile = None
            for i, field in enumerate(corr[4 * t:4 * t + 4]):
                piece = field[:, 128 * (k // 4):128 * (k // 4) + 128]
                turn = (i - k) % 4
                piece = pltpu.roll(piece, width * turn, axis=1) if turn else piece
                tile = piece if tile is None else jnp.where(lane == i, piece, tile)
            back_out[k, t] = tile
    returned = []
    for j in range(1, n_gy):
        peer = at(0, j)
        returned.append(message(22 + j, back_out.at[peer[1]], back_in.at[gy], peer))
    for copy in returned:
        copy.start()
    back_in[gy] = back_out[gy]

    def shift_up(u, c, p, direction):
        return u[c, p + 1] if direction == 0 else y_up(u[c, p]) if direction == 1 else z_up(u[c, p])

    def curl(c, p):
        a, b = (c + 1) % 3, (c + 2) % 3
        return (shift_up(sm, b, p, a) - sm[b, p]) - (shift_up(sm, a, p, b) - sm[a, p])

    new = {key: tt[key] + curl(*key) for key in tt}
    div3 = {p: divergence(new, p) for p in range(-1, 2)}
    for c in range(3):
        for p in range(2):
            key = (c, p)
            out = new[key] + damping * (rr[key] - apply_faces(new, div3, c, p)) / dd[key]
            vel_ref[c, p] = out[0:8]

    for copy in returned:
        copy.wait_recv()
    for t in range(2):
        whole = back_in[:, t].reshape(rows, 128)
        for i in range(4 if t == 0 else 2):
            c, p = divmod(4 * t + i, 2)
            piece = whole if i == 0 else pltpu.roll(whole, 128 - width * i, axis=1)
            ec_ref[c, p] = piece[:, :width]
    for copy in first + exchange + edge_halo + second + returned:
        copy.wait_send()


def on_device(right_side, face_mass, edge_scale, edge_mass, node_scale):
    n_gx, n_gy = lax.axis_size("gx"), lax.axis_size("gy")
    nz = right_side.shape[3]

    def tiles(*lead):
        return pltpu.VMEM((*lead, 8, nz), jnp.float32)

    def packed(*lead):
        return pltpu.VMEM((*lead, 8, 128), jnp.float32)

    vmem = pl.BlockSpec(memory_space=pltpu.VMEM)
    count = 23 + n_gy - 1
    return pl.pallas_call(
        functools.partial(kernel, n_gx, n_gy),
        out_shape=(jax.ShapeDtypeStruct(right_side.shape, jnp.float32),
                   jax.ShapeDtypeStruct(edge_scale.shape, jnp.float32)),
        in_specs=[vmem] * 5,
        out_specs=(vmem, vmem),
        scratch_shapes=[
            tiles(9), tiles(5), tiles(6), tiles(6), tiles(5), tiles(5), tiles(3), tiles(3),
            packed(n_gy, 7), packed(n_gy, 2),
            tiles(9), tiles(5), tiles(6), tiles(6), tiles(5), tiles(5), tiles(3), tiles(3),
            packed(n_gy, 7), packed(n_gy, 2),
            pltpu.VMEM((2, 7, 16, nz), jnp.float32),
            tiles(5), tiles(9), tiles(5), tiles(9),
            tiles(8), tiles(5), tiles(8), tiles(5),
            tiles(1), tiles(1), tiles(1),
            pltpu.SemaphoreType.DMA((count,)), pltpu.SemaphoreType.DMA((count,)),
        ],
        compiler_params=pltpu.CompilerParams(
            collective_id=0, has_side_effects=True, vmem_limit_bytes=32 * 1024 * 1024),
    )(right_side, face_mass, edge_scale, edge_mass, node_scale)


def solution(mesh):
    placed = (
        P(None, "gx", "gy", None),
        P(None, "gx", "gy", None),
        P(None, "gx", None, "gy"),
        P(None, "gx", None, "gy"),
        P("gx", None, "gy"),
    )
    return jax.shard_map(
        on_device,
        mesh=mesh,
        in_specs=placed,
        out_specs=(P(None, "gx", "gy", None), P(None, "gx", None, "gy")),
        check_vma=False,
    )
```

time: 227 us -> 53.1 us (0.23)
  starting transfers between devices: 133 us -> 0 us
  waiting for transfers between devices: 71.5 us -> 0 us
  Pallas kernels: 0 us -> 47.6 us
  local copies, waits for them, and re-layouts: 12.2 us -> 4.09 us
  other arithmetic: 5.79 us -> 0 us
    ppermute x28 -> x0, starting transfers between devices: 114 us -> none  [the longest x14 60.5 us: with_halo(): lax.ppermute(head, axis, [((i + 1) % count, i) for i in range(count)])]
    ppermute x28 -> x0, waiting for transfers between devices: 60.9 us -> none  [the longest x14 58.2 us: with_halo(): lax.ppermute(tail, axis, [(i, (i + 1) % count) for i in range(count)])]
    pallas_call x0 -> x1, Pallas kernels: none -> 47.6 us  [on_device(): pl.pallas_call(functools.partial(kernel, n_gx, n_gy), out_shape=(jax.Shap...]
    all_to_all x2 -> x0, starting transfers between devices: 19 us -> none  [the longest x1 10 us: on_device(): lax.all_to_all(edge_residual, 'gy', split_axis=3, concat_axis=2, tiled=True)]
    all_to_all x2 -> x0, waiting for transfers between devices: 10.6 us -> none  [the longest x1 5.33 us: to_faces(): return lax.all_to_all(edges, 'gy', split_axis=2, concat_axis=3, tiled=True)]
    unnamed x22 -> x12, local copies, waits for them, and re-layouts: 7.3 us -> 3.32 us
  transfers between devices with their start and end apart: 30 -> 0, of which waited for: 16 -> 0; matrix products, arithmetic and copies ran while one was open for 2% -> 0% of each run, Pallas kernels for 0% -> 0%
where the time goes in v1:
time: 53.1 us; the launch traced here: 52.3 us
  Pallas kernels  47.6 us (90%)
  local copies, waits for them, and re-layouts  4.09 us (8%)
  between operations  0.67 us (1%)
    pallas_call x1, Pallas kernels, on_device(): pl.pallas_call(functools.partial(kernel, n_gx, n_gy), out_shape=(jax.Shap...  47.6 us
    unnamed x12, local copies, waits for them, and re-layouts  3.32 us

profile of v1, /device:TPU:6, one launch (start us, length us, event | category | flops | bytes accessed | tf_op | source)
XLA Modules:
  0.0 52.3 jit_solution(5417402228701788592)
XLA Ops:
  0.6 0.0 copy-start.2
  0.6 0.9 %copy.9.ns_ref = f32[2,96,32]{2,1,0:T(8,128)S(1)} copy(f32[2,96,32]{1,2,0:T(8,128)} %param.9) | data formatting | bytes 49152 | tf_op args[4]
  1.5 0.0 copy-done.2
  1.5 0.0 copy-start.3
  1.5 0.1 copy.7.es_ref
  1.7 0.7 %copy-done.3 = f32[3,2,96,32]{2,3,1,0:T(8,128)S(1)} copy-done((f32[3,2,96,32]{2,3,1,0:T(8,128)S(1)}, f32[3,2,96,32]{2,3,1,0:T(8,128)}, u32[]{:S(2)}) %copy-start.3) | copy-done | bytes 73752
  2.4 0.0 copy-start
  2.4 0.0 copy-start.1
  2.4 0.1 copy.8.em_ref
  2.6 0.7 %copy-done = f32[3,2,8,384]{3,2,1,0:T(8,128)S(1)} copy-done((f32[3,2,8,384]{3,2,1,0:T(8,128)S(1)}, f32[3,2,8,384]{3,2,1,0:T(8,128)}, u32[]{:S(2)}) %copy-start) | copy-done | bytes 73752
  3.3 0.0 copy-done.1
  3.4 47.6 %shard_map.68 = (f32[3,2,8,384]{3,2,1,0:T(8,128)S(1)}, f32[3,2,96,32]{3,2,1,0:T(8,128)S(1)}) custom-call(f32[3,2,8,384]{3,2,1,0:T(8,128)S(1)} %copy-done, f32[3,2,8,384]{3,2,1,0:T(8,128)S(1)} %copy-done.1, f32[3,2,96,32]{3,2,1,0:T(8,128)S(1)} %copy.7.es_ref, f32[3,2,96,32]{3,2,1,0:T(8,128)S(1)} %copy.8.em_ref, f32[2,96,32]{2,1,0:T(8,128)S(1)} %copy.9.ns_ref), custom_call_target="tpu_custom_call" | custom-call | tf_op jit(solution)/shard_map/pallas_call | solution.py:305
  50.9 0.8 %copy.10 = f32[3,2,96,32]{2,3,1,0:T(8,128)} copy(f32[3,2,96,32]{3,2,1,0:T(8,128)S(1)} %get-tuple-element.3) | data formatting | bytes 147456 | tf_op jit(solution)/shard_map/pallas_call | solution.py:305
  51.7 0.6 %copy.12 = f32[3,2,8,384]{3,2,1,0:T(8,128)} copy(f32[3,2,8,384]{3,2,1,0:T(8,128)S(1)} %get-tuple-element.6) | data formatting | bytes 147456
Async XLA Ops:
  0.6 0.9 %copy-start.2 = (f32[3,2,96,32]{2,3,1,0:T(8,128)S(1)}, f32[3,2,96,32]{2,3,1,0:T(8,128)}, u32[]{:S(2)}) copy-start(f32[3,2,96,32]{2,3,1,0:T(8,128)} %param.7) | copy-start | bytes 221188
  1.5 0.9 %copy-start.3 = (f32[3,2,96,32]{2,3,1,0:T(8,128)S(1)}, f32[3,2,96,32]{2,3,1,0:T(8,128)}, u32[]{:S(2)}) copy-start(f32[3,2,96,32]{2,3,1,0:T(8,128)} %param.8) | copy-start | bytes 221188
  2.4 0.9 %copy-start = (f32[3,2,8,384]{3,2,1,0:T(8,128)S(1)}, f32[3,2,8,384]{3,2,1,0:T(8,128)}, u32[]{:S(2)}) copy-start(f32[3,2,8,384]{3,2,1,0:T(8,128)} %r_ref.1) | copy-start | bytes 221188
  2.4 0.9 %copy-start.1 = (f32[3,2,8,384]{3,2,1,0:T(8,128)S(1)}, f32[3,2,8,384]{3,2,1,0:T(8,128)}, u32[]{:S(2)}) copy-start(f32[3,2,8,384]{3,2,1,0:T(8,128)} %fm_ref.1) | copy-start | bytes 221188

commit v2 on v0

v2 whole, which is shorter than its diff:
```python
import functools

import jax
import jax.numpy as jnp
from jax import lax
from jax.experimental import pallas as pl
from jax.experimental.pallas import tpu as pltpu
from jax.sharding import PartitionSpec as P

MESH = pl.DeviceIdType.MESH
grad_div_weight = 1.0
damping = 0.3


def up(a, axis):
    return pltpu.roll(a, a.shape[axis] - 1, axis=axis)


def down(a, axis):
    return pltpu.roll(a, 1, axis=axis)


def half_turn(a):
    return pltpu.roll(a, 4, axis=0)


def sublane(shape):
    return lax.broadcasted_iota(jnp.int32, shape, len(shape) - 2)


def shift_up(u, c, p, direction, axes):
    return u[c, p + 1] if direction == 0 else up(u[c, p], axes[direction - 1])


def shift_down(u, c, p, direction, axes):
    return u[c, p - 1] if direction == 0 else down(u[c, p], axes[direction - 1])


FACE = (0, 1)
EDGE = (1, 0)


def curl(u, c, p, axes):
    a, b = (c + 1) % 3, (c + 2) % 3
    return (shift_up(u, b, p, a, axes) - u[b, p]) - (shift_up(u, a, p, b, axes) - u[a, p])


def curl_adjoint(g, a, p, axes):
    b, c = (a + 1) % 3, (a + 2) % 3
    return (shift_down(g, b, p, c, axes) - g[b, p]) - (shift_down(g, c, p, b, axes) - g[c, p])


def turn(a, by):
    return pltpu.roll(a, by % 8, axis=0) if by % 8 else a


def pack_rows(items):
    packed = []
    for base in range(0, len(items), 8):
        tile = None
        for slot, (a, row) in enumerate(items[base:base + 8]):
            piece = turn(a, slot - row)
            tile = piece if tile is None else jnp.where(sublane(a.shape) == slot, piece, tile)
        packed.append(tile)
    return packed


def with_rows(tile, *items):
    for ref, slot, row in items:
        piece = turn(ref[slot // 8], row - slot % 8)
        tile = piece if tile is None else jnp.where(sublane(piece.shape) == row, piece, tile)
    return tile


def joined(own_part, halo):
    return jnp.concatenate([own_part, halo], axis=0)


def kernel(n_gx, n_gy, r_hbm, fm_hbm, es_hbm, em_hbm, ns_hbm, vel_ref, ec_ref,
           r_ref, fm_ref, es_ref, em_ref, ns_ref,
           x_right, x_left, y_upper, y_lower, cr_upper, cr_lower, cl_upper, cl_lower,
           in_left, in_right, in_below, in_above, in_cl_below, in_cl_above, in_cr_below, in_cr_above,
           es_out, es_in, faced, ef_right, ef_left, in_ef_left, in_ef_right,
           e_left, e_right, e_next, e_prev, e_ca, e_cb, in_e_right, in_e_left, in_e_next, in_e_prev, in_e_ca, in_e_cb,
           res_right, res_left, res_upper, res_lower, rr_upper, rr_lower, rl_upper, rl_lower,
           in_res_left, in_res_right, in_res_below, in_res_above, in_rl_below, in_rl_above, in_rr_below, in_rr_above, win, in_win, in_win_right, in_win_left,
           load_sem, send_sem, recv_sem):
    gx, gy = lax.axis_index("gx"), lax.axis_index("gy")

    def at(dx, dy):
        return (lax.rem(gx + dx + n_gx, n_gx), lax.rem(gy + dy + n_gy, n_gy))

    barrier = pltpu.get_barrier_semaphore()
    greeted = [at(a, b) for a in (1, -1) for b in (-1, 0, 1)] + [at(0, j) for j in range(1, n_gy)]
    for peer in greeted:
        pl.semaphore_signal(barrier, inc=1, device_id=peer, device_id_type=MESH)
    loads = [pltpu.make_async_copy(src, dst, load_sem.at[i]) for i, (src, dst) in enumerate(
        ((r_hbm, r_ref), (fm_hbm, fm_ref), (es_hbm, es_ref), (em_hbm, em_ref), (ns_hbm, ns_ref)))]
    for load in loads:
        load.start()
    sent = []

    def message(src, dst, peer):
        index = len(sent)
        copy = pltpu.make_async_remote_copy(
            src_ref=src, dst_ref=dst, send_sem=send_sem.at[index], recv_sem=recv_sem.at[index],
            device_id=peer, device_id_type=MESH)
        sent.append(copy)
        copy.start()
        return copy

    for load in loads[:2]:
        load.wait()
    r = [[r_ref[c, p] for p in range(2)] for c in range(3)]
    fm = [[fm_ref[c, p] for p in range(2)] for c in range(3)]
    s1 = [[damping * r[c][p] / (fm[c][p] + 2.0 * grad_div_weight) for p in range(2)] for c in range(3)]
    known = [s1[0][1] - s1[0][0], up(s1[2][0], 1) - s1[2][0]]
    wide = sublane(known[0].shape)
    partial = known[0] + (jnp.where(wide == 7, 0.0, up(s1[1][0], 0)) - s1[1][0]) + known[1]
    to_right = [r[c][1] for c in range(3)] + [fm[c][1] for c in range(3)] + [partial]
    to_left = [r[0][0], fm[0][0], known[0] + known[1], s1[1][0]]
    cells = [(c, p) for c in range(3) for p in range(2)]
    for ref, parts in (
            (x_right, to_right), (x_left, to_left),
            (y_upper, pack_rows([(f[c][p], 7) for f in (r, fm) for c, p in cells] + [(s1[c][p], 6) for c, p in cells])),
            (y_lower, pack_rows([(f[p], 0) for f in (r[1], fm[1], s1[0], s1[2]) for p in range(2)]
                                + [(s1[1][p], 1) for p in range(2)])),
            (cr_upper, pack_rows([(s1[c][1], 7) for c in range(3)])),
            (cr_lower, pack_rows([(r[1][1], 0), (fm[1][1], 0), (s1[0][1], 0), (s1[2][1], 0), (s1[1][1], 1), (s1[1][0], 0)])),
            (cl_upper, pack_rows([(to_left[i], 7) for i in range(4)] + [(s1[0][0], 6)])),
            (cl_lower, pack_rows([(s1[1][0], 0), (s1[0][0], 0)]))):
        for i, part in enumerate(parts):
            ref[i] = part

    for load in loads[2:]:
        load.wait()
    nz, ny = es_ref.shape[2], es_ref.shape[3]

    def wrapped(field):
        return jnp.concatenate([field, field[:, :16], field[:, ny - 16:]], axis=1)

    es = {(c, p): wrapped(es_ref[c, p]) for c in range(3) for p in range(2)}
    em = {(c, p): wrapped(em_ref[c, p]) for c in range(3) for p in range(2)}
    ns = {p: wrapped(ns_ref[p]) for p in range(2)}
    both = {key: em[key] * es[key] for key in es}
    for i, field in enumerate([both[c, 0] for c in range(3)] + [ns[0]]):
        e_left[i] = field
    e_right[0] = both[0, 1]
    for i, field in enumerate([both[key] for key in cells] + [ns[0], ns[1]]):
        e_next[i] = field[0:8]
    for p in range(2):
        e_prev[p] = both[2, p][nz - 8:]
    e_ca[0] = both[2, 0][nz - 8:]
    e_cb[0] = both[0, 1][0:8]

    order = [(c, p) for p in range(2) for c in range(3)]
    sub = sublane((8, 128))
    halos = []
    for t in range(2):
        group = [es[key] for key in order[4 * t:4 * t + 4]]
        group += [group[0]] * (4 - len(group))
        turned = jnp.concatenate(group, axis=0).T
        es_out[:, t] = turned[:ny].reshape(n_gy, 8, 128)
        after = turned[8:ny + 8].reshape(n_gy, 8, 128)
        before = jnp.concatenate([turned[ny - 8:ny], turned[:ny - 8]], axis=0).reshape(n_gy, 8, 128)
        halos.append((after, before))
    for k in range(n_gy):
        first_halo = jnp.where(sub < 4, halos[0][0][k], halos[0][1][k])
        second_halo = half_turn(jnp.where(sub < 4, halos[1][0][k], halos[1][1][k]))
        es_out[k, 2] = jnp.where((sub == 3) | (sub == 4), second_halo, first_halo)

    pl.semaphore_wait(barrier, len(greeted))

    first = [
        message(cr_upper, in_cl_below, at(1, 1)), message(cr_lower, in_cl_above, at(1, -1)),
        message(cl_upper, in_cr_below, at(-1, 1)), message(cl_lower, in_cr_above, at(-1, -1)),
        message(x_left, in_right, at(-1, 0)), message(x_right, in_left, at(1, 0)),
        message(y_upper, in_below, at(0, 1)), message(y_lower, in_above, at(0, -1)),
    ]
    exchange = []
    for j in range(1, n_gy):
        peer = at(0, j)
        exchange.append(message(es_out.at[peer[1]], es_in.at[gy], peer))
    es_in[gy] = es_out[gy]
    edge_halo = [
        message(e_left, in_e_right, at(-1, 0)), message(e_right, in_e_left, at(1, 0)),
        message(e_next, in_e_next, at(0, -1)), message(e_prev, in_e_prev, at(0, 1)),
        message(e_ca, in_e_ca, at(-1, 1)), message(e_cb, in_e_cb, at(1, -1)),
    ]

    for copy in first:
        copy.wait_recv()

    rr, ff, dd, ss = {}, {}, {}, {}
    for i, (c, p) in enumerate(cells):
        above = c == 1
        rr[c, p] = joined(r_ref[c, p], with_rows(None, (in_below, i, 7), *[(in_above, p, 0)] * above))
        ff[c, p] = joined(fm_ref[c, p], with_rows(None, (in_below, 6 + i, 7), *[(in_above, 2 + p, 0)] * above))
    for c in range(3):
        rr[c, -1] = joined(in_left[c], with_rows(None, (in_cl_above, 0, 0)) if c == 1 else in_left[c])
        ff[c, -1] = joined(in_left[3 + c], with_rows(None, (in_cl_above, 1, 0)) if c == 1 else in_left[3 + c])
    rr[0, 2] = joined(in_right[0], with_rows(None, (in_cr_below, 0, 7)))
    ff[0, 2] = joined(in_right[1], with_rows(None, (in_cr_below, 1, 7)))
    for key in rr:
        dd[key] = ff[key] + 2.0 * grad_div_weight
        ss[key] = damping * rr[key] / dd[key]

    def more_rows(key, *items):
        ss[key] = joined(ss[key][0:8], with_rows(ss[key][8:16], *items))

    for i, (c, p) in enumerate(cells):
        more_rows((c, p), (in_below, 12 + i, 6), (in_above, (4, 8, 6)[c] + p, 1 if c == 1 else 0))
    for c in range(3):
        more_rows((c, -1), (in_cl_below, c, 7), (in_cl_above, (2, 4, 3)[c], 1 if c == 1 else 0))
    more_rows((0, 2), (in_cr_below, 4, 6), (in_cr_above, 1, 0))
    known = joined(in_right[2], with_rows(None, (in_cr_below, 2, 7)))
    second_flux = joined(in_right[3], with_rows(None, (in_cr_below, 3, 7), (in_cr_above, 0, 0)))

    def divergence(u, p):
        return (u[0, p + 1] - u[0, p]) + (up(u[1, p], 0) - u[1, p]) + (up(u[2, p], 1) - u[2, p])

    def apply_faces(u, div, c, p):
        shifted = div[p - 1] if c == 0 else down(div[p], c - 1)
        return ff[c, p] * u[c, p] + grad_div_weight * (shifted - div[p])

    div1 = {p: divergence(ss, p) for p in range(-1, 2)}
    div1[2] = known + (up(second_flux, 0) - second_flux)
    far = in_left[6]
    far = jnp.where(wide == 7, far + turn(in_cl_above[0], 2), far)
    div1[-2] = joined(far, far)
    tt = {key: ss[key] + damping * (rr[key] - apply_faces(ss, div1, *key)) / dd[key] for key in rr}
    div2 = {p: divergence(tt, p) for p in range(-1, 2)}
    res = {(c, p): rr[c, p] - apply_faces(tt, div2, c, p) for c in range(3) for p in range(2)}

    mine = {key: res[key][0:8] for key in res}
    for ref, parts in (
            (res_right, [mine[1, 0], mine[2, 0], mine[0, 1], mine[1, 1], mine[2, 1]]),
            (res_left, [mine[0, 0], mine[1, 0], mine[2, 0]]),
            (res_upper, pack_rows([(mine[key], 7) for key in cells] + [(mine[c, p], 6) for c in (0, 2) for p in range(2)])),
            (res_lower, pack_rows([(mine[key], 0) for key in cells])),
            (rr_upper, pack_rows([(mine[c, 1], 7) for c in range(3)])),
            (rr_lower, pack_rows([(mine[c, 1], 0) for c in range(3)] + [(mine[1, 0], 0)])),
            (rl_upper, pack_rows([(mine[c, 0], 7) for c in range(3)] + [(mine[0, 0], 6)])),
            (rl_lower, pack_rows([(mine[c, 0], 0) for c in range(2)]))):
        for i, part in enumerate(parts):
            ref[i] = part
    second = [
        message(rr_upper, in_rl_below, at(1, 1)), message(rr_lower, in_rl_above, at(1, -1)),
        message(rl_upper, in_rr_below, at(-1, 1)), message(rl_lower, in_rr_above, at(-1, -1)),
        message(res_right, in_res_left, at(1, 0)), message(res_left, in_res_right, at(-1, 0)),
        message(res_upper, in_res_below, at(0, 1)), message(res_lower, in_res_above, at(0, -1)),
    ]

    span = nz + 8
    lane = lax.broadcasted_iota(jnp.int32, (8, 128), 1)
    total = r_ref.shape[3]
    for k in range(n_gy):
        for p in range(2):
            tile = None
            for c in range(3):
                shift = (span * c - (nz * k - 4)) % total
                piece = (pltpu.roll(mine[c, p], shift, axis=1) if shift else mine[c, p])[:, :128]
                tile = piece if tile is None else jnp.where(lane >= span * c, piece, tile)
            win[k, p] = tile
    windows = []
    for j in range(n_gy):
        for side, p, dst in ((1, 1, in_win_left), (-1, 0, in_win_right)):
            peer = at(side, j)
            windows.append(message(win.at[peer[1], p], dst.at[gy], peer))
    for j in range(1, n_gy):
        peer = at(0, j)
        windows.append(message(win.at[peer[1]], in_win.at[gy], peer))
    in_win[gy] = win[gy]

    for copy in exchange:
        copy.wait_recv()
    lane4 = lane // nz
    for i, (c, p) in enumerate(order):
        t, q = divmod(i, 4)
        for m in range(total // 128):
            for h in range(2):
                tile = None
                for jj in range(4):
                    piece = es_in[4 * m + jj, 2 if h else t]
                    if jj != q:
                        piece = pltpu.roll(piece, (nz * (jj - q)) % 128, axis=1)
                    tile = piece if tile is None else jnp.where(lane4 == jj, piece, tile)
                faced[p, c, 8 * h:8 * h + 8, 128 * m:128 * m + 128] = half_turn(tile) if h and t else tile
    for ref, p, comps in ((ef_right, 1, (0, 1, 2)), (ef_left, 0, (1, 2))):
        tile = None
        for i, c in enumerate(comps):
            ref[i] = faced[p, c, 0:8]
            piece = faced[p, c, 8:16]
            piece = pltpu.roll(piece, 2 * i, axis=0) if i else piece
            tile = piece if tile is None else jnp.where((wide == 2 * i) | (wide == 2 * i - 1), piece, tile)
        ref[len(comps)] = tile
    scale_halo = [message(ef_right, in_ef_left, at(1, 0)), message(ef_left, in_ef_right, at(-1, 0))]

    for copy in second + scale_halo:
        copy.wait_recv()

    def ef_halo(ref, count, i):
        tile = ref[count]
        return joined(ref[i], pltpu.roll(tile, 8 - 2 * i, axis=0) if i else tile)

    for i, (c, p) in enumerate(cells):
        rows = [(in_res_below, i, 7), (in_res_above, i, 0)] + [(in_res_below, 6 + c + p, 6)] * (c != 1)
        res[c, p] = joined(mine[c, p], with_rows(None, *rows))
    res[1, -2] = joined(in_res_left[0], with_rows(None, (in_rl_above, 3, 0)))
    res[2, -2] = joined(in_res_left[1], in_res_left[1])
    for c in range(3):
        res[c, -1] = joined(in_res_left[2 + c], with_rows(None, (in_rl_below, c, 7), (in_rl_above, c, 0)))
        rows = [(in_rr_below, c, 7)] + [(in_rr_below, 3, 6)] * (c == 0) + [(in_rr_above, c, 0)] * (c < 2)
        res[c, 2] = joined(in_res_right[c], with_rows(None, *rows))
    scale = {(c, p): faced[p, c] for c in range(3) for p in range(2)}
    for c in range(3):
        scale[c, -1] = ef_halo(in_ef_left, 3, c)
    for c in range(1, 3):
        scale[c, 2] = ef_halo(in_ef_right, 2, c - 1)
    sm = {key: scale[key] * curl_adjoint(res, *key, FACE) for key in scale}
    new = {key: tt[key] + curl(sm, *key, FACE) for key in tt}
    div3 = {p: divergence(new, p) for p in range(-1, 2)}
    for c in range(3):
        for p in range(2):
            key = (c, p)
            out = new[key] + damping * (rr[key] - apply_faces(new, div3, c, p)) / dd[key]
            vel_ref[c, p] = out[0:8]

    for copy in edge_halo + windows:
        copy.wait_recv()
    g = {}
    for p, ref in ((-1, in_win_left), (0, None), (1, None), (2, in_win_right)):
        rows = (in_win[:, p] if ref is None else ref[...]).reshape(ny, 128)
        turned = jnp.concatenate([rows, rows[:16], rows[ny - 16:]], axis=0).T
        for c in range(3):
            g[c, p] = pltpu.roll(turned[span * c:span * c + span], span - 4, axis=0)
    low = sub < 4
    both = {}
    for i, (c, p) in enumerate(cells):
        halo = in_e_next[i]
        if c == 2:
            halo = jnp.where(low, halo, in_e_prev[p])
        both[c, p] = joined(wrapped(em_ref[c, p]) * wrapped(es_ref[c, p]), halo)
    node = {p: joined(wrapped(ns_ref[p]), in_e_next[6 + p]) for p in range(2)}
    both[0, -1] = joined(in_e_left[0], in_e_cb[0])
    for c in range(3):
        both[c, 2] = joined(in_e_right[c], in_e_ca[0])
    node[2] = joined(in_e_right[3], in_e_ca[0])
    edge_residual = {key: curl_adjoint(g, *key, EDGE) for key in both}
    ww = {key: both[key] * edge_residual[key] for key in both}
    pot = {}
    for p in range(3):
        adjoint = ((ww[0, p - 1] - ww[0, p]) + (down(ww[1, p], 1) - ww[1, p])) + (down(ww[2, p], 0) - ww[2, p])
        pot[0, p] = node[p] * -adjoint
    for c in range(3):
        for p in range(2):
            ahead = pot[0, p + 1] if c == 0 else up(pot[0, p], EDGE[c - 1])
            smoothed = wrapped(es_ref[c, p]) * edge_residual[c, p][:nz]
            ec_ref[c, p] = (smoothed + (ahead - pot[0, p])[:nz])[:, :ny]
    for copy in sent:
        copy.wait_send()


def on_device(right_side, face_mass, edge_scale, edge_mass, node_scale):
    n_gx, n_gy = lax.axis_size("gx"), lax.axis_size("gy")
    edge_scale, edge_mass, node_scale = (jnp.swapaxes(a, -1, -2) for a in (edge_scale, edge_mass, node_scale))
    total, nz = right_side.shape[3], edge_scale.shape[2]

    def own(a):
        return pltpu.VMEM(a.shape, jnp.float32)

    def rows(*lead):
        return pltpu.VMEM((*lead, 8, total), jnp.float32)

    def tile(*lead):
        return pltpu.VMEM((*lead, 8, 128), jnp.float32)

    def field(*lead):
        return pltpu.VMEM((*lead, nz, 128), jnp.float32)

    vmem = pl.BlockSpec(memory_space=pltpu.VMEM)
    arguments = (right_side, face_mass, edge_scale, edge_mass, node_scale)
    first = [rows(7), rows(4), rows(3), rows(2), rows(1), rows(1), rows(1), rows(1)]
    second = [rows(5), rows(3), rows(2), rows(1), rows(1), rows(1), rows(1), rows(1)]
    halo = [field(4), field(1), tile(8), tile(2), tile(1), tile(1)]
    count = 24 + 5 * n_gy - 2
    velocity, correction = pl.pallas_call(
        functools.partial(kernel, n_gx, n_gy),
        out_shape=(jax.ShapeDtypeStruct(right_side.shape, jnp.float32),
                   jax.ShapeDtypeStruct(edge_scale.shape, jnp.float32)),
        in_specs=[pl.BlockSpec(memory_space=pltpu.HBM)] * 5,
        out_specs=(vmem, vmem),
        scratch_shapes=[own(a) for a in arguments] + first + first + [
            tile(n_gy, 3), tile(n_gy, 3), pltpu.VMEM((2, 3, 16, total), jnp.float32),
            rows(4), rows(3), rows(4), rows(3)] + halo + halo + [
            *second, *second, tile(n_gy, 2), tile(n_gy, 2), tile(n_gy), tile(n_gy),
            pltpu.SemaphoreType.DMA((5,)),
            pltpu.SemaphoreType.DMA((count,)), pltpu.SemaphoreType.DMA((count,)),
        ],
        compiler_params=pltpu.CompilerParams(
            collective_id=0, has_side_effects=True, vmem_limit_bytes=60 * 1024 * 1024),
    )(*arguments)
    return velocity, jnp.swapaxes(correction, 2, 3)


def solution(mesh):
    placed = (
        P(None, "gx", "gy", None),
        P(None, "gx", "gy", None),
        P(None, "gx", None, "gy"),
        P(None, "gx", None, "gy"),
        P("gx", None, "gy"),
    )
    return jax.shard_map(
        on_device,
        mesh=mesh,
        in_specs=placed,
        out_specs=(P(None, "gx", "gy", None), P(None, "gx", None, "gy")),
        check_vma=False,
    )
```

time: 227 us -> 43.2 us (0.19); the launches traced: 224 us -> 42.9 us
  starting transfers between devices: 133 us -> 0 us
  waiting for transfers between devices: 71.5 us -> 0 us
  Pallas kernels: 0 us -> 40.1 us
  local copies, waits for them, and re-layouts: 12.2 us -> 2.2 us
  other arithmetic: 5.79 us -> 0 us
    ppermute x28 -> x0, starting transfers between devices: 114 us -> none  [the longest x14 60.5 us: with_halo(): lax.ppermute(head, axis, [((i + 1) % count, i) for i in range(count)])]
    ppermute x28 -> x0, waiting for transfers between devices: 60.9 us -> none  [the longest x14 58.2 us: with_halo(): lax.ppermute(tail, axis, [(i, (i + 1) % count) for i in range(count)])]
    pallas_call x0 -> x1, Pallas kernels: none -> 40.1 us  [on_device(): pl.pallas_call(functools.partial(kernel, n_gx, n_gy), out_shape=(jax.Shap...]
    all_to_all x2 -> x0, starting transfers between devices: 19 us -> none  [the longest x1 10 us: on_device(): lax.all_to_all(edge_residual, 'gy', split_axis=3, concat_axis=2, tiled=True)]
    all_to_all x2 -> x0, waiting for transfers between devices: 10.6 us -> none  [the longest x1 5.33 us: to_faces(): return lax.all_to_all(edges, 'gy', split_axis=2, concat_axis=3, tiled=True)]
    unnamed x22 -> x4, local copies, waits for them, and re-layouts: 7.3 us -> 2.2 us
  transfers between devices with their start and end apart: 30 -> 0, of which waited for: 16 -> 0; matrix products, arithmetic and copies ran while one was open for 2% -> 0% of each run, Pallas kernels for 0% -> 0%
where the time goes in v2:
time: 43.2 us; the launch traced here: 42.9 us
  Pallas kernels  40.1 us (93%)
  local copies, waits for them, and re-layouts  2.2 us (5%)
  between operations  0.65 us (2%)
    pallas_call x1, Pallas kernels, on_device(): pl.pallas_call(functools.partial(kernel, n_gx, n_gy), out_shape=(jax.Shap...  40.1 us
    unnamed x4, local copies, waits for them, and re-layouts  2.2 us

profile of v2, /device:TPU:6, one launch (start us, length us, event | category | flops | bytes accessed | tf_op | source)
XLA Modules:
  0.0 42.9 jit_solution(718939567927752387)
XLA Ops:
  0.6 40.1 %shard_map.68 = (f32[3,2,8,384]{3,2,1,0:T(8,128)}, f32[3,2,32,96]{3,2,1,0:T(8,128)}) custom-call(f32[3,2,8,384]{3,2,1,0:T(8,128)} %r_hbm.1, f32[3,2,8,384]{3,2,1,0:T(8,128)} %fm_hbm.1, f32[3,2,32,96]{3,2,1,0:T(8,128)} %bitcast.5, f32[3,2,32,96]{3,2,1,0:T(8,128)} %bitcast.6, f32[2,32,96]{2,1,0:T(8,128)} %bitcast.7), custom_call_target="tpu_custom_call" | custom-call | tf_op jit(solution)/shard_map/pallas_call | solution.py:387
  40.7 0.0 copy-start
  40.7 1.6 %copy.9 = f32[3,2,8,384]{3,2,1,0:T(8,128)} copy(f32[3,2,8,384]{3,2,1,0:T(8,128)} %get-tuple-element.8) | data formatting | bytes 147456
  42.3 0.0 copy-done
  42.3 0.6 %copy.10 = f32[3,2,96,32]{2,3,1,0:T(8,128)} copy(f32[3,2,96,32]{2,3,1,0:T(8,128)S(1)} %bitcast.4) | data formatting | bytes 147456
Async XLA Ops:
  40.7 1.6 %copy-start = (f32[3,2,32,96]{3,2,1,0:T(8,128)S(1)}, f32[3,2,32,96]{3,2,1,0:T(8,128)}, u32[]{:S(2)}) copy-start(f32[3,2,32,96]{3,2,1,0:T(8,128)} %get-tuple-element.5) | copy-start | bytes 221188

commit v3 on v2

--- a/solution.py
+++ b/solution.py
@@ -76,8 +76,8 @@
     return jnp.concatenate([own_part, halo], axis=0)
 
 
-def kernel(n_gx, n_gy, r_hbm, fm_hbm, es_hbm, em_hbm, ns_hbm, vel_ref, ec_ref,
-           r_ref, fm_ref, es_ref, em_ref, ns_ref,
+def kernel(n_gx, n_gy, r_hbm, fm_hbm, es_hbm, em_hbm, ns_hbm, vel_hbm, ec_hbm,
+           r_ref, fm_ref, es_ref, em_ref, ns_ref, vel_ref, ec_ref,
            x_right, x_left, y_upper, y_lower, cr_upper, cr_lower, cl_upper, cl_lower,
            in_left, in_right, in_below, in_above, in_cl_below, in_cl_above, in_cr_below, in_cr_above,
            es_out, es_in, faced, ef_right, ef_left, in_ef_left, in_ef_right,
@@ -142,16 +142,16 @@
     es = {(c, p): wrapped(es_ref[c, p]) for c in range(3) for p in range(2)}
     em = {(c, p): wrapped(em_ref[c, p]) for c in range(3) for p in range(2)}
     ns = {p: wrapped(ns_ref[p]) for p in range(2)}
-    both = {key: em[key] * es[key] for key in es}
-    for i, field in enumerate([both[c, 0] for c in range(3)] + [ns[0]]):
+    products = {key: em[key] * es[key] for key in es}
+    for i, field in enumerate([products[c, 0] for c in range(3)] + [ns[0]]):
         e_left[i] = field
-    e_right[0] = both[0, 1]
-    for i, field in enumerate([both[key] for key in cells] + [ns[0], ns[1]]):
+    e_right[0] = products[0, 1]
+    for i, field in enumerate([products[key] for key in cells] + [ns[0], ns[1]]):
         e_next[i] = field[0:8]
     for p in range(2):
-        e_prev[p] = both[2, p][nz - 8:]
-    e_ca[0] = both[2, 0][nz - 8:]
-    e_cb[0] = both[0, 1][0:8]
+        e_prev[p] = products[2, p][nz - 8:]
+    e_ca[0] = products[2, 0][nz - 8:]
+    e_cb[0] = products[0, 1][0:8]
 
     order = [(c, p) for p in range(2) for c in range(3)]
     sub = sublane((8, 128))
@@ -178,7 +178,7 @@
         message(y_upper, in_below, at(0, 1)), message(y_lower, in_above, at(0, -1)),
     ]
     exchange = []
-    for j in range(1, n_gy):
+    for j in [k for k in sorted(range(n_gy), key=lambda j: (abs(j % 4 - 2), -min(j, n_gy - j))) if k]:
         peer = at(0, j)
         exchange.append(message(es_out.at[peer[1]], es_in.at[gy], peer))
     es_in[gy] = es_out[gy]
@@ -263,13 +263,13 @@
                 tile = piece if tile is None else jnp.where(lane >= span * c, piece, tile)
             win[k, p] = tile
     windows = []
-    for j in range(n_gy):
+    for j in [k for k in sorted(range(n_gy), key=lambda j: (abs(j % 4 - 2), -min(j, n_gy - j))) if k]:
+        peer = at(0, j)
+        windows.append(message(win.at[peer[1]], in_win.at[gy], peer))
+    for j in sorted(range(n_gy), key=lambda j: (abs(j % 4 - 2), -min(j, n_gy - j))):
         for side, p, dst in ((1, 1, in_win_left), (-1, 0, in_win_right)):
             peer = at(side, j)
             windows.append(message(win.at[peer[1], p], dst.at[gy], peer))
-    for j in range(1, n_gy):
-        peer = at(0, j)
-        windows.append(message(win.at[peer[1]], in_win.at[gy], peer))
     in_win[gy] = win[gy]
 
     for copy in exchange:
@@ -296,44 +296,8 @@
         ref[len(comps)] = tile
     scale_halo = [message(ef_right, in_ef_left, at(1, 0)), message(ef_left, in_ef_right, at(-1, 0))]
 
-    for copy in second + scale_halo:
+    for copy in edge_halo:
         copy.wait_recv()
-
-    def ef_halo(ref, count, i):
-        tile = ref[count]
-        return joined(ref[i], pltpu.roll(tile, 8 - 2 * i, axis=0) if i else tile)
-
-    for i, (c, p) in enumerate(cells):
-        rows = [(in_res_below, i, 7), (in_res_above, i, 0)] + [(in_res_below, 6 + c + p, 6)] * (c != 1)
-        res[c, p] = joined(mine[c, p], with_rows(None, *rows))
-    res[1, -2] = joined(in_res_left[0], with_rows(None, (in_rl_above, 3, 0)))
-    res[2, -2] = joined(in_res_left[1], in_res_left[1])
-    for c in range(3):
-        res[c, -1] = joined(in_res_left[2 + c], with_rows(None, (in_rl_below, c, 7), (in_rl_above, c, 0)))
-        rows = [(in_rr_below, c, 7)] + [(in_rr_below, 3, 6)] * (c == 0) + [(in_rr_above, c, 0)] * (c < 2)
-        res[c, 2] = joined(in_res_right[c], with_rows(None, *rows))
-    scale = {(c, p): faced[p, c] for c in range(3) for p in range(2)}
-    for c in range(3):
-        scale[c, -1] = ef_halo(in_ef_left, 3, c)
-    for c in range(1, 3):
-        scale[c, 2] = ef_halo(in_ef_right, 2, c - 1)
-    sm = {key: scale[key] * curl_adjoint(res, *key, FACE) for key in scale}
-    new = {key: tt[key] + curl(sm, *key, FACE) for key in tt}
-    div3 = {p: divergence(new, p) for p in range(-1, 2)}
-    for c in range(3):
-        for p in range(2):
-            key = (c, p)
-            out = new[key] + damping * (rr[key] - apply_faces(new, div3, c, p)) / dd[key]
-            vel_ref[c, p] = out[0:8]
-
-    for copy in edge_halo + windows:
-        copy.wait_recv()
-    g = {}
-    for p, ref in ((-1, in_win_left), (0, None), (1, None), (2, in_win_right)):
-        rows = (in_win[:, p] if ref is None else ref[...]).reshape(ny, 128)
-        turned = jnp.concatenate([rows, rows[:16], rows[ny - 16:]], axis=0).T
-        for c in range(3):
-            g[c, p] = pltpu.roll(turned[span * c:span * c + span], span - 4, axis=0)
     low = sub < 4
     both = {}
     for i, (c, p) in enumerate(cells):
@@ -346,6 +310,46 @@
     for c in range(3):
         both[c, 2] = joined(in_e_right[c], in_e_ca[0])
     node[2] = joined(in_e_right[3], in_e_ca[0])
+    for copy in second + scale_halo:
+        copy.wait_recv()
+
+    def ef_halo(ref, count, i):
+        tile = ref[count]
+        return joined(ref[i], pltpu.roll(tile, 8 - 2 * i, axis=0) if i else tile)
+
+    for i, (c, p) in enumerate(cells):
+        rows = [(in_res_below, i, 7), (in_res_above, i, 0)] + [(in_res_below, 6 + c + p, 6)] * (c != 1)
+        res[c, p] = joined(mine[c, p], with_rows(None, *rows))
+    res[1, -2] = joined(in_res_left[0], with_rows(None, (in_rl_above, 3, 0)))
+    res[2, -2] = joined(in_res_left[1], in_res_left[1])
+    for c in range(3):
+        res[c, -1] = joined(in_res_left[2 + c], with_rows(None, (in_rl_below, c, 7), (in_rl_above, c, 0)))
+        rows = [(in_rr_below, c, 7)] + [(in_rr_below, 3, 6)] * (c == 0) + [(in_rr_above, c, 0)] * (c < 2)
+        res[c, 2] = joined(in_res_right[c], with_rows(None, *rows))
+    scale = {(c, p): faced[p, c] for c in range(3) for p in range(2)}
+    for c in range(3):
+        scale[c, -1] = ef_halo(in_ef_left, 3, c)
+    for c in range(1, 3):
+        scale[c, 2] = ef_halo(in_ef_right, 2, c - 1)
+    sm = {key: scale[key] * curl_adjoint(res, *key, FACE) for key in scale}
+    new = {key: tt[key] + curl(sm, *key, FACE) for key in tt}
+    div3 = {p: divergence(new, p) for p in range(-1, 2)}
+    for c in range(3):
+        for p in range(2):
+            key = (c, p)
+            out = new[key] + damping * (rr[key] - apply_faces(new, div3, c, p)) / dd[key]
+            vel_ref[c, p] = out[0:8]
+
+    store = [pltpu.make_async_copy(vel_ref, vel_hbm, load_sem.at[5]), pltpu.make_async_copy(ec_ref, ec_hbm, load_sem.at[6])]
+    store[0].start()
+    for copy in windows:
+        copy.wait_recv()
+    g = {}
+    for p, ref in ((-1, in_win_left), (0, None), (1, None), (2, in_win_right)):
+        rows = (in_win[:, p] if ref is None else ref[...]).reshape(ny, 128)
+        turned = jnp.concatenate([rows, rows[:16], rows[ny - 16:]], axis=0).T
+        for c in range(3):
+            g[c, p] = pltpu.roll(turned[span * c:span * c + span], span - 4, axis=0)
     edge_residual = {key: curl_adjoint(g, *key, EDGE) for key in both}
     ww = {key: both[key] * edge_residual[key] for key in both}
     pot = {}
@@ -357,8 +361,16 @@
             ahead = pot[0, p + 1] if c == 0 else up(pot[0, p], EDGE[c - 1])
             smoothed = wrapped(es_ref[c, p]) * edge_residual[c, p][:nz]
             ec_ref[c, p] = (smoothed + (ahead - pot[0, p])[:nz])[:, :ny]
+    store[1].start()
     for copy in sent:
         copy.wait_send()
+    for copy in store:
+        copy.wait()
+
+
+def hand_over(a, b, a_out, b_out):
+    a_out[...] = a[...]
+    b_out[...] = b[...]
 
 
 def on_device(right_side, face_mass, edge_scale, edge_mass, node_scale):
@@ -378,7 +390,6 @@
     def field(*lead):
         return pltpu.VMEM((*lead, nz, 128), jnp.float32)
 
-    vmem = pl.BlockSpec(memory_space=pltpu.VMEM)
     arguments = (right_side, face_mass, edge_scale, edge_mass, node_scale)
     first = [rows(7), rows(4), rows(3), rows(2), rows(1), rows(1), rows(1), rows(1)]
     second = [rows(5), rows(3), rows(2), rows(1), rows(1), rows(1), rows(1), rows(1)]
@@ -389,17 +400,26 @@
         out_shape=(jax.ShapeDtypeStruct(right_side.shape, jnp.float32),
                    jax.ShapeDtypeStruct(edge_scale.shape, jnp.float32)),
         in_specs=[pl.BlockSpec(memory_space=pltpu.HBM)] * 5,
-        out_specs=(vmem, vmem),
-        scratch_shapes=[own(a) for a in arguments] + first + first + [
+        out_specs=(pl.BlockSpec(memory_space=pl.ANY),) * 2,
+        scratch_shapes=[own(a) for a in (*arguments, right_side, edge_scale)] + first + first + [
             tile(n_gy, 3), tile(n_gy, 3), pltpu.VMEM((2, 3, 16, total), jnp.float32),
             rows(4), rows(3), rows(4), rows(3)] + halo + halo + [
             *second, *second, tile(n_gy, 2), tile(n_gy, 2), tile(n_gy), tile(n_gy),
-            pltpu.SemaphoreType.DMA((5,)),
+            pltpu.SemaphoreType.DMA((7,)),
             pltpu.SemaphoreType.DMA((count,)), pltpu.SemaphoreType.DMA((count,)),
         ],
         compiler_params=pltpu.CompilerParams(
             collective_id=0, has_side_effects=True, vmem_limit_bytes=60 * 1024 * 1024),
     )(*arguments)
+    inside = pl.BlockSpec(memory_space=pltpu.VMEM)
+    velocity, correction = pl.pallas_call(
+        hand_over,
+        out_shape=(jax.ShapeDtypeStruct(velocity.shape, jnp.float32),
+                   jax.ShapeDtypeStruct(correction.shape, jnp.float32)),
+        in_specs=[inside, inside],
+        out_specs=(inside, inside),
+        compiler_params=pltpu.CompilerParams(vmem_limit_bytes=60 * 1024 * 1024),
+    )(velocity, correction)
     return velocity, jnp.swapaxes(correction, 2, 3)
 
 

time: 43.2 us -> 42.2 us (0.977)
  local copies, waits for them, and re-layouts: 2.2 us -> 0 us
  Pallas kernels: 40.1 us -> 40.9 us
    unnamed x4 -> x0, local copies, waits for them, and re-layouts: 2.2 us -> none
    pallas_call x0 -> x1, Pallas kernels: none -> 1.6 us  [on_device(): pl.pallas_call(hand_over, out_shape=(jax.ShapeDtypeStruct(velocity.shape,...]
    pallas_call x1, Pallas kernels: 40.1 us -> 39.3 us  [on_device(): pl.pallas_call(functools.partial(kernel, n_gx, n_gy), out_shape=(jax.Shap...]
where the time goes in v3:
time: 42.2 us; the launch traced here: 41.5 us
  Pallas kernels  40.9 us (97%)
  between operations  0.64 us (2%)
    pallas_call x1, Pallas kernels, on_device(): pl.pallas_call(functools.partial(kernel, n_gx, n_gy), out_shape=(jax.Shap...  39.3 us
    pallas_call x1, Pallas kernels, on_device(): pl.pallas_call(hand_over, out_shape=(jax.ShapeDtypeStruct(velocity.shape,...  1.6 us

profile of v3, /device:TPU:6, one launch (start us, length us, event | category | flops | bytes accessed | tf_op | source)
XLA Modules:
  0.0 41.5 jit_solution(6673715285251047790)
XLA Ops:
  0.6 39.3 %shard_map.68 = (f32[3,2,8,384]{3,2,1,0:T(8,128)}, f32[3,2,32,96]{3,2,1,0:T(8,128)}) custom-call(f32[3,2,8,384]{3,2,1,0:T(8,128)} %r_hbm.1, f32[3,2,8,384]{3,2,1,0:T(8,128)} %fm_hbm.1, f32[3,2,32,96]{3,2,1,0:T(8,128)} %bitcast.4, f32[3,2,32,96]{3,2,1,0:T(8,128)} %bitcast.5, f32[2,32,96]{2,1,0:T(8,128)} %bitcast.6), custom_call_target="tpu_custom_call" | custom-call | tf_op jit(solution)/shard_map/pallas_call | solution.py:398
  39.9 1.6 %shard_map.69 = (f32[3,2,8,384]{3,2,1,0:T(8,128)}, f32[3,2,32,96]{3,2,1,0:T(8,128)}) custom-call(f32[3,2,8,384]{3,2,1,0:T(8,128)} %get-tuple-element.6.a, f32[3,2,32,96]{3,2,1,0:T(8,128)} %get-tuple-element.7.b), custom_call_target="tpu_custom_call" | custom-call | tf_op jit(solution)/shard_map/pallas_call | solution.py:415

commit v4 on v3

--- a/solution.py
+++ b/solution.py
@@ -233,6 +233,23 @@
     res = {(c, p): rr[c, p] - apply_faces(tt, div2, c, p) for c in range(3) for p in range(2)}
 
     mine = {key: res[key][0:8] for key in res}
+    span = nz + 8
+    lane = lax.broadcasted_iota(jnp.int32, (8, 128), 1)
+    total = r_ref.shape[3]
+    for k in range(n_gy):
+        for p in range(2):
+            tile = None
+            for c in range(3):
+                shift = (span * c - (nz * k - 4)) % total
+                piece = (pltpu.roll(mine[c, p], shift, axis=1) if shift else mine[c, p])[:, :128]
+                tile = piece if tile is None else jnp.where(lane >= span * c, piece, tile)
+            win[k, p] = tile
+    windows = []
+    for j in [k for k in sorted(range(n_gy), key=lambda j: (abs(j % 4 - 2), -min(j, n_gy - j))) if k]:
+        peer = at(0, j)
+        windows.append(message(win.at[peer[1]], in_win.at[gy], peer))
+    in_win[gy] = win[gy]
+
     for ref, parts in (
             (res_right, [mine[1, 0], mine[2, 0], mine[0, 1], mine[1, 1], mine[2, 1]]),
             (res_left, [mine[0, 0], mine[1, 0], mine[2, 0]]),
@@ -251,26 +268,6 @@
         message(res_upper, in_res_below, at(0, 1)), message(res_lower, in_res_above, at(0, -1)),
     ]
 
-    span = nz + 8
-    lane = lax.broadcasted_iota(jnp.int32, (8, 128), 1)
-    total = r_ref.shape[3]
-    for k in range(n_gy):
-        for p in range(2):
-            tile = None
-            for c in range(3):
-                shift = (span * c - (nz * k - 4)) % total
-                piece = (pltpu.roll(mine[c, p], shift, axis=1) if shift else mine[c, p])[:, :128]
-                tile = piece if tile is None else jnp.where(lane >= span * c, piece, tile)
-            win[k, p] = tile
-    windows = []
-    for j in [k for k in sorted(range(n_gy), key=lambda j: (abs(j % 4 - 2), -min(j, n_gy - j))) if k]:
-        peer = at(0, j)
-        windows.append(message(win.at[peer[1]], in_win.at[gy], peer))
-    for j in sorted(range(n_gy), key=lambda j: (abs(j % 4 - 2), -min(j, n_gy - j))):
-        for side, p, dst in ((1, 1, in_win_left), (-1, 0, in_win_right)):
-            peer = at(side, j)
-            windows.append(message(win.at[peer[1], p], dst.at[gy], peer))
-    in_win[gy] = win[gy]
 
     for copy in exchange:
         copy.wait_recv()
@@ -296,8 +293,9 @@
         ref[len(comps)] = tile
     scale_halo = [message(ef_right, in_ef_left, at(1, 0)), message(ef_left, in_ef_right, at(-1, 0))]
 
-    for copy in edge_halo:
+    for copy in windows + edge_halo:
         copy.wait_recv()
+    passed_on = [message(in_win.at[:, 1], in_win_left, at(1, 0)), message(in_win.at[:, 0], in_win_right, at(-1, 0))]
     low = sub < 4
     both = {}
     for i, (c, p) in enumerate(cells):
@@ -342,7 +340,7 @@
 
     store = [pltpu.make_async_copy(vel_ref, vel_hbm, load_sem.at[5]), pltpu.make_async_copy(ec_ref, ec_hbm, load_sem.at[6])]
     store[0].start()
-    for copy in windows:
+    for copy in passed_on:
         copy.wait_recv()
     g = {}
     for p, ref in ((-1, in_win_left), (0, None), (1, None), (2, in_win_right)):

time: 42.2 us -> 40.6 us (0.962)
  the two profiles are of different devices: /device:TPU:6 before, /device:TPU:4 now
where the time goes in v4:
time: 40.6 us; the launch traced here: 40.4 us
  Pallas kernels  39.8 us (98%)
  between operations  0.64 us (2%)
    pallas_call x1, Pallas kernels, on_device(): pl.pallas_call(functools.partial(kernel, n_gx, n_gy), out_shape=(jax.Shap...  38.2 us
    pallas_call x1, Pallas kernels, on_device(): pl.pallas_call(hand_over, out_shape=(jax.ShapeDtypeStruct(velocity.shape,...  1.6 us

profile of v4, /device:TPU:4, one launch (start us, length us, event | category | flops | bytes accessed | tf_op | source)
XLA Modules:
  0.0 40.4 jit_solution(9907047633937864113)
XLA Ops:
  0.6 38.2 %shard_map.68 = (f32[3,2,8,384]{3,2,1,0:T(8,128)}, f32[3,2,32,96]{3,2,1,0:T(8,128)}) custom-call(f32[3,2,8,384]{3,2,1,0:T(8,128)} %r_hbm.1, f32[3,2,8,384]{3,2,1,0:T(8,128)} %fm_hbm.1, f32[3,2,32,96]{3,2,1,0:T(8,128)} %bitcast.4, f32[3,2,32,96]{3,2,1,0:T(8,128)} %bitcast.5, f32[2,32,96]{2,1,0:T(8,128)} %bitcast.6), custom_call_target="tpu_custom_call" | custom-call | tf_op jit(solution)/shard_map/pallas_call | solution.py:396
  38.8 1.6 %shard_map.69 = (f32[3,2,8,384]{3,2,1,0:T(8,128)}, f32[3,2,32,96]{3,2,1,0:T(8,128)}) custom-call(f32[3,2,8,384]{3,2,1,0:T(8,128)} %get-tuple-element.6.a, f32[3,2,32,96]{3,2,1,0:T(8,128)} %get-tuple-element.7.b), custom_call_target="tpu_custom_call" | custom-call | tf_op jit(solution)/shard_map/pallas_call | solution.py:413

commit v5 on v4

--- a/solution.py
+++ b/solution.py
@@ -146,10 +146,8 @@
     for i, field in enumerate([products[c, 0] for c in range(3)] + [ns[0]]):
         e_left[i] = field
     e_right[0] = products[0, 1]
-    for i, field in enumerate([products[key] for key in cells] + [ns[0], ns[1]]):
-        e_next[i] = field[0:8]
-    for p in range(2):
-        e_prev[p] = products[2, p][nz - 8:]
+    e_next[0] = pack_rows([(field[0:8], 0) for field in [products[key] for key in cells] + [ns[0], ns[1]]])[0]
+    e_prev[0] = pack_rows([(products[2, p][nz - 8:], 7) for p in range(2)])[0]
     e_ca[0] = products[2, 0][nz - 8:]
     e_cb[0] = products[0, 1][0:8]
 
@@ -164,10 +162,13 @@
         after = turned[8:ny + 8].reshape(n_gy, 8, 128)
         before = jnp.concatenate([turned[ny - 8:ny], turned[:ny - 8]], axis=0).reshape(n_gy, 8, 128)
         halos.append((after, before))
+    column = lax.broadcasted_iota(jnp.int32, (8, 128), 1)
     for k in range(n_gy):
-        first_halo = jnp.where(sub < 4, halos[0][0][k], halos[0][1][k])
-        second_halo = half_turn(jnp.where(sub < 4, halos[1][0][k], halos[1][1][k]))
-        es_out[k, 2] = jnp.where((sub == 3) | (sub == 4), second_halo, first_halo)
+        upper = jnp.where(sub < 4, halos[0][0][k], halos[0][1][k])
+        lower = jnp.where(sub < 4, halos[1][0][k], halos[1][1][k])
+        spare = jnp.where((sub == 1) | (sub == 2), turn(upper, 2), pltpu.roll(upper, 2 * nz, axis=1))
+        spare = jnp.where((sub == 3) | (sub == 4), half_turn(pltpu.roll(lower, 2 * nz, axis=1)), spare)
+        es_out[k, 1] = jnp.where(column < 2 * nz, es_out[k, 1], spare)
 
     pl.semaphore_wait(barrier, len(greeted))
 
@@ -187,6 +188,32 @@
         message(e_next, in_e_next, at(0, -1)), message(e_prev, in_e_prev, at(0, 1)),
         message(e_ca, in_e_ca, at(-1, 1)), message(e_cb, in_e_cb, at(1, -1)),
     ]
+
+    for copy in exchange:
+        copy.wait_recv()
+    lane4 = lax.broadcasted_iota(jnp.int32, (8, 128), 1) // nz
+    total = r_ref.shape[3]
+    for i, (c, p) in enumerate(order):
+        t, q = divmod(i, 4)
+        for m in range(total // 128):
+            for h in range(2):
+                tile = None
+                for jj in range(4):
+                    piece = es_in[4 * m + jj, 1 if h else t]
+                    place = 2 + i % 2 if h else q
+                    if jj != place:
+                        piece = pltpu.roll(piece, (nz * (jj - place)) % 128, axis=1)
+                    tile = piece if tile is None else jnp.where(lane4 == jj, piece, tile)
+                faced[p, c, 8 * h:8 * h + 8, 128 * m:128 * m + 128] = turn(tile, -2 * (i // 2)) if h else tile
+    for ref, p, comps in ((ef_right, 1, (0, 1, 2)), (ef_left, 0, (1, 2))):
+        tile = None
+        for i, c in enumerate(comps):
+            ref[i] = faced[p, c, 0:8]
+            piece = faced[p, c, 8:16]
+            piece = pltpu.roll(piece, 2 * i, axis=0) if i else piece
+            tile = piece if tile is None else jnp.where((wide == 2 * i) | (wide == 2 * i - 1), piece, tile)
+        ref[len(comps)] = tile
+    scale_halo = [message(ef_right, in_ef_left, at(1, 0)), message(ef_left, in_ef_right, at(-1, 0))]
 
     for copy in first:
         copy.wait_recv()
@@ -269,41 +296,14 @@
     ]
 
 
-    for copy in exchange:
-        copy.wait_recv()
-    lane4 = lane // nz
-    for i, (c, p) in enumerate(order):
-        t, q = divmod(i, 4)
-        for m in range(total // 128):
-            for h in range(2):
-                tile = None
-                for jj in range(4):
-                    piece = es_in[4 * m + jj, 2 if h else t]
-                    if jj != q:
-                        piece = pltpu.roll(piece, (nz * (jj - q)) % 128, axis=1)
-                    tile = piece if tile is None else jnp.where(lane4 == jj, piece, tile)
-                faced[p, c, 8 * h:8 * h + 8, 128 * m:128 * m + 128] = half_turn(tile) if h and t else tile
-    for ref, p, comps in ((ef_right, 1, (0, 1, 2)), (ef_left, 0, (1, 2))):
-        tile = None
-        for i, c in enumerate(comps):
-            ref[i] = faced[p, c, 0:8]
-            piece = faced[p, c, 8:16]
-            piece = pltpu.roll(piece, 2 * i, axis=0) if i else piece
-            tile = piece if tile is None else jnp.where((wide == 2 * i) | (wide == 2 * i - 1), piece, tile)
-        ref[len(comps)] = tile
-    scale_halo = [message(ef_right, in_ef_left, at(1, 0)), message(ef_left, in_ef_right, at(-1, 0))]
-
     for copy in windows + edge_halo:
         copy.wait_recv()
     passed_on = [message(in_win.at[:, 1], in_win_left, at(1, 0)), message(in_win.at[:, 0], in_win_right, at(-1, 0))]
-    low = sub < 4
     both = {}
     for i, (c, p) in enumerate(cells):
-        halo = in_e_next[i]
-        if c == 2:
-            halo = jnp.where(low, halo, in_e_prev[p])
-        both[c, p] = joined(wrapped(em_ref[c, p]) * wrapped(es_ref[c, p]), halo)
-    node = {p: joined(wrapped(ns_ref[p]), in_e_next[6 + p]) for p in range(2)}
+        places = [(in_e_next, i, 0)] + [(in_e_prev, p, 7)] * (c == 2)
+        both[c, p] = joined(wrapped(em_ref[c, p]) * wrapped(es_ref[c, p]), with_rows(None, *places))
+    node = {p: joined(wrapped(ns_ref[p]), with_rows(None, (in_e_next, 6 + p, 0))) for p in range(2)}
     both[0, -1] = joined(in_e_left[0], in_e_cb[0])
     for c in range(3):
         both[c, 2] = joined(in_e_right[c], in_e_ca[0])
@@ -391,7 +391,7 @@
     arguments = (right_side, face_mass, edge_scale, edge_mass, node_scale)
     first = [rows(7), rows(4), rows(3), rows(2), rows(1), rows(1), rows(1), rows(1)]
     second = [rows(5), rows(3), rows(2), rows(1), rows(1), rows(1), rows(1), rows(1)]
-    halo = [field(4), field(1), tile(8), tile(2), tile(1), tile(1)]
+    halo = [field(4), field(1), tile(1), tile(1), tile(1), tile(1)]
     count = 24 + 5 * n_gy - 2
     velocity, correction = pl.pallas_call(
         functools.partial(kernel, n_gx, n_gy),
@@ -400,7 +400,7 @@
         in_specs=[pl.BlockSpec(memory_space=pltpu.HBM)] * 5,
         out_specs=(pl.BlockSpec(memory_space=pl.ANY),) * 2,
         scratch_shapes=[own(a) for a in (*arguments, right_side, edge_scale)] + first + first + [
-            tile(n_gy, 3), tile(n_gy, 3), pltpu.VMEM((2, 3, 16, total), jnp.float32),
+            tile(n_gy, 2), tile(n_gy, 2), pltpu.VMEM((2, 3, 16, total), jnp.float32),
             rows(4), rows(3), rows(4), rows(3)] + halo + halo + [
             *second, *second, tile(n_gy, 2), tile(n_gy, 2), tile(n_gy), tile(n_gy),
             pltpu.SemaphoreType.DMA((7,)),

time: 40.6 us -> 40 us (0.985)
  the two profiles are of different devices: /device:TPU:4 before, /device:TPU:6 now
where the time goes in v5:
time: 40 us; the launch traced here: 39.8 us
  Pallas kernels  39.2 us (98%)
  between operations  0.64 us (2%)
    pallas_call x1, Pallas kernels, on_device(): pl.pallas_call(functools.partial(kernel, n_gx, n_gy), out_shape=(jax.Shap...  37.6 us
    pallas_call x1, Pallas kernels, on_device(): pl.pallas_call(hand_over, out_shape=(jax.ShapeDtypeStruct(velocity.shape,...  1.6 us

profile of v5, /device:TPU:6, one launch (start us, length us, event | category | flops | bytes accessed | tf_op | source)
XLA Modules:
  0.0 39.8 jit_solution(16955739922971337296)
XLA Ops:
  0.6 37.6 %shard_map.68 = (f32[3,2,8,384]{3,2,1,0:T(8,128)}, f32[3,2,32,96]{3,2,1,0:T(8,128)}) custom-call(f32[3,2,8,384]{3,2,1,0:T(8,128)} %r_hbm.1, f32[3,2,8,384]{3,2,1,0:T(8,128)} %fm_hbm.1, f32[3,2,32,96]{3,2,1,0:T(8,128)} %bitcast.4, f32[3,2,32,96]{3,2,1,0:T(8,128)} %bitcast.5, f32[2,32,96]{2,1,0:T(8,128)} %bitcast.6), custom_call_target="tpu_custom_call" | custom-call | tf_op jit(solution)/shard_map/pallas_call | solution.py:396
  38.2 1.6 %shard_map.69 = (f32[3,2,8,384]{3,2,1,0:T(8,128)}, f32[3,2,32,96]{3,2,1,0:T(8,128)}) custom-call(f32[3,2,8,384]{3,2,1,0:T(8,128)} %get-tuple-element.6.a, f32[3,2,32,96]{3,2,1,0:T(8,128)} %get-tuple-element.7.b), custom_call_target="tpu_custom_call" | custom-call | tf_op jit(solution)/shard_map/pallas_call | solution.py:413

commit v6 on v5

--- a/solution.py
+++ b/solution.py
@@ -296,9 +296,11 @@
     ]
 
 
-    for copy in windows + edge_halo:
+    for copy in windows:
         copy.wait_recv()
     passed_on = [message(in_win.at[:, 1], in_win_left, at(1, 0)), message(in_win.at[:, 0], in_win_right, at(-1, 0))]
+    for copy in edge_halo:
+        copy.wait_recv()
     both = {}
     for i, (c, p) in enumerate(cells):
         places = [(in_e_next, i, 0)] + [(in_e_prev, p, 7)] * (c == 2)

time: 40 us -> 40 us (level)
  no operation moved by 1% of the time
where the time goes in v6:
time: 40 us; the launch traced here: 39.8 us
  Pallas kernels  39.2 us (98%)
  between operations  0.64 us (2%)
    pallas_call x1, Pallas kernels, on_device(): pl.pallas_call(functools.partial(kernel, n_gx, n_gy), out_shape=(jax.Shap...  37.6 us
    pallas_call x1, Pallas kernels, on_device(): pl.pallas_call(hand_over, out_shape=(jax.ShapeDtypeStruct(velocity.shape,...  1.6 us

profile of v6, /device:TPU:6, one launch (start us, length us, event | category | flops | bytes accessed | tf_op | source)
XLA Modules:
  0.0 39.8 jit_solution(4542320004528400678)
XLA Ops:
  0.6 37.6 %shard_map.68 = (f32[3,2,8,384]{3,2,1,0:T(8,128)}, f32[3,2,32,96]{3,2,1,0:T(8,128)}) custom-call(f32[3,2,8,384]{3,2,1,0:T(8,128)} %r_hbm.1, f32[3,2,8,384]{3,2,1,0:T(8,128)} %fm_hbm.1, f32[3,2,32,96]{3,2,1,0:T(8,128)} %bitcast.4, f32[3,2,32,96]{3,2,1,0:T(8,128)} %bitcast.5, f32[2,32,96]{2,1,0:T(8,128)} %bitcast.6), custom_call_target="tpu_custom_call" | custom-call | tf_op jit(solution)/shard_map/pallas_call | solution.py:398
  38.2 1.6 %shard_map.69 = (f32[3,2,8,384]{3,2,1,0:T(8,128)}, f32[3,2,32,96]{3,2,1,0:T(8,128)}) custom-call(f32[3,2,8,384]{3,2,1,0:T(8,128)} %get-tuple-element.6.a, f32[3,2,32,96]{3,2,1,0:T(8,128)} %get-tuple-element.7.b), custom_call_target="tpu_custom_call" | custom-call | tf_op jit(solution)/shard_map/pallas_call | solution.py:415

commit v7 on v6

--- a/solution.py
+++ b/solution.py
@@ -175,7 +175,7 @@
     first = [
         message(cr_upper, in_cl_below, at(1, 1)), message(cr_lower, in_cl_above, at(1, -1)),
         message(cl_upper, in_cr_below, at(-1, 1)), message(cl_lower, in_cr_above, at(-1, -1)),
-        message(x_left, in_right, at(-1, 0)), message(x_right, in_left, at(1, 0)),
+        message(x_right, in_left, at(1, 0)), message(x_left, in_right, at(-1, 0)),
         message(y_upper, in_below, at(0, 1)), message(y_lower, in_above, at(0, -1)),
     ]
     exchange = []

time: 40 us -> 40 us (level)
  no operation moved by 1% of the time
where the time goes in v7:
time: 40 us; the launch traced here: 39.8 us
  Pallas kernels  39.2 us (98%)
  between operations  0.64 us (2%)
    pallas_call x1, Pallas kernels, on_device(): pl.pallas_call(functools.partial(kernel, n_gx, n_gy), out_shape=(jax.Shap...  37.6 us
    pallas_call x1, Pallas kernels, on_device(): pl.pallas_call(hand_over, out_shape=(jax.ShapeDtypeStruct(velocity.shape,...  1.6 us

profile of v7, /device:TPU:6, one launch (start us, length us, event | category | flops | bytes accessed | tf_op | source)
XLA Modules:
  0.0 39.8 jit_solution(15036858312575499447)
XLA Ops:
  0.6 37.6 %shard_map.68 = (f32[3,2,8,384]{3,2,1,0:T(8,128)}, f32[3,2,32,96]{3,2,1,0:T(8,128)}) custom-call(f32[3,2,8,384]{3,2,1,0:T(8,128)} %r_hbm.1, f32[3,2,8,384]{3,2,1,0:T(8,128)} %fm_hbm.1, f32[3,2,32,96]{3,2,1,0:T(8,128)} %bitcast.4, f32[3,2,32,96]{3,2,1,0:T(8,128)} %bitcast.5, f32[2,32,96]{2,1,0:T(8,128)} %bitcast.6), custom_call_target="tpu_custom_call" | custom-call | tf_op jit(solution)/shard_map/pallas_call | solution.py:398
  38.2 1.6 %shard_map.69 = (f32[3,2,8,384]{3,2,1,0:T(8,128)}, f32[3,2,32,96]{3,2,1,0:T(8,128)}) custom-call(f32[3,2,8,384]{3,2,1,0:T(8,128)} %get-tuple-element.6.a, f32[3,2,32,96]{3,2,1,0:T(8,128)} %get-tuple-element.7.b), custom_call_target="tpu_custom_call" | custom-call | tf_op jit(solution)/shard_map/pallas_call | solution.py:415
